TPU v7x, 128 devices: a whole 4x4x4 slice. The times are simulated.
128 devices in a mesh: row: 32 (over y_hi, z, x), col: 4 (over y_lo, core).
Axes of the slice: x: 4, y: 4 (y_hi: 2, y_lo: 2; y = y_hi * 2 + y_lo), z: 4, core: 2. Of those that a mesh axis runs over, the one named last changes fastest.
Arguments:
- layer_input: bfloat16 [16384, 1088], P('row', 'col'), may hold values from -32 to 32
- first_norm_gain: float32 [1088], P('col'), may hold values from 0.5 to 1.5
- first_norm_bias: float32 [1088], P('col'), may hold values from -1.5 to 1.5
- w_qkv: bfloat16 [1088, 3264], P('row', 'col'), may hold values from -0.7276069 to 0.7276069
- w_out: bfloat16 [1088, 1088], P('col', 'row'), may hold values from -3 to 3
- second_norm_gain: float32 [1088], P('col'), may hold values from 0.5 to 1.5
- second_norm_bias: float32 [1088], P('col'), may hold values from -1.5 to 1.5
- w_up: bfloat16 [1088, 4352], P('row', 'col'), may hold values from -0.1875 to 0.1875
- w_down: bfloat16 [4352, 1088], P('col', 'row'), may hold values from -0.09375 to 0.09375
- gradient_of_output: bfloat16 [16384, 1088], P('row', 'col'), may hold values from -6 to 6
Outputs:
- layer_output: bfloat16 [16384, 1088], P('row', 'col')
- gradient_of_input: float32 [16384, 1088], P('row', 'col')
- first_gain_gradient: float32 [1088], P('col')
- grad_norm1_bias: float32 [1088], P('col')
- grad_w_qkv: float32 [1088, 3264], P('row', 'col')
- grad_w_out: float32 [1088, 1088], P('col', 'row')
- second_gain_gradient: float32 [1088], P('col')
- grad_norm2_bias: float32 [1088], P('col')
- grad_w_up: float32 [1088, 4352], P('row', 'col')
- grad_w_down: float32 [4352, 1088], P('col', 'row')
All inputs are finite; a program needn't handle non-finite values.
Results may differ from a plain program's by a relative error of at most 0.025.
Values may be sent and summed in bfloat16 or wider, within the bound.
A program may use at most 128 MiB of HBM per device.

v0:
```python
import math

import jax
import jax.numpy as jnp
from jax import lax
from jax.experimental import pallas as pl
from jax.experimental.pallas import tpu as pltpu
from jax.sharding import PartitionSpec as P

HEADS = 17
HEAD_DIM = 64
D = 1088
SEQ = 2048
MAIN = 1024
WIDE = 1152
PACK = 1280
QKV_COLS = 816
QUARTER = 128
PAIR = 256
KEYS = 512

gelu_coef = math.sqrt(2.0 / math.pi)
norm_epsilon = 1e-05
masked_score = -1e30
MESH = pl.DeviceIdType.MESH
F32 = jnp.float32
BF16 = jnp.bfloat16
VMEM_LIMIT = 60 * 1024 * 1024
ANY = pl.BlockSpec(memory_space=pl.ANY)
VMEM_SPEC = pl.BlockSpec(memory_space=pltpu.VMEM)
SMEM_SPEC = pl.BlockSpec(memory_space=pltpu.SMEM)

GATHER_ORDERS = (("x", "y", "z"), ("y", "z", "x"), ("z", "x", "y"))
SCATTER_ORDERS = (("z", "y", "x"), ("x", "z", "y"), ("y", "x", "z"))


def dot_nn(a, b):
    return lax.dot_general(a, b, (((1,), (0,)), ((), ())), preferred_element_type=F32)


def dot_nt(a, b):
    return lax.dot_general(a, b, (((1,), (1,)), ((), ())), preferred_element_type=F32)


class Place:
    def __init__(self):
        self.row = lax.axis_index("row")
        self.col = lax.axis_index("col")
        self.at = {
            "x": lax.rem(self.row, 4),
            "z": lax.rem(self.row // 4, 4),
            "y": (self.row // 16) * 2 + self.col // 2,
        }
        self.core = lax.rem(self.col, 2)

    def device(self, at, core):
        return ((at["y"] // 2) * 16 + at["z"] * 4 + at["x"], lax.rem(at["y"], 2) * 2 + core)

    def step(self, axis, distance):
        at = dict(self.at)
        at[axis] = lax.rem(at[axis] + distance + 4, 4)
        return self.device(at, self.core)

    def partner(self):
        return (self.row, self.col + 1 - 2 * self.core)

    def beside(self, distance):
        return (self.row, lax.rem(self.col + distance, 4))

    def neighbours(self):
        found = [self.step(axis, d) for axis in ("x", "y", "z") for d in (1, -1)]
        found.append(self.partner())
        other = lax.rem(self.col // 2 + 1, 2)
        found.append((self.row, other * 2 + 1 - self.core))
        return found


def greet(devices):
    barrier = pltpu.get_barrier_semaphore()
    for device in devices:
        pl.semaphore_signal(barrier, inc=1, device_id=device, device_id_type=MESH)
    pl.semaphore_wait(barrier, len(devices))


def everything():
    return slice(None)


def place_index(fixed):
    if "y" in fixed:
        y_lo, y_hi = lax.rem(fixed["y"], 2), fixed["y"] // 2
    else:
        y_lo, y_hi = everything(), everything()
    return (y_lo, y_hi, fixed.get("z", everything()), fixed.get("x", everything()))


def remote(source, target, ssem, rsem, device):
    return pltpu.make_async_remote_copy(
        src_ref=source, dst_ref=target, send_sem=ssem, recv_sem=rsem,
        device_id=device, device_id_type=MESH,
    )


def gather_kernel(
    block0, block1, block2, x_ref, g_ref, v_ref,
    all0, all1, all2, x_out, g_out, v_out,
    send, recv, last_send, last_recv, local, in_send, in_recv, in_local,
):
    me = Place()
    blocks = (block0, block1, block2)
    wholes = (all0, all1, all2)
    greet(me.neighbours())

    def region(piece, fixed, rows=None):
        index = place_index(fixed) + ((everything(),) if rows is None else (pl.ds(rows, 16),))
        return wholes[piece].at[index]

    def around(piece, stage, value):
        order = GATHER_ORDERS[piece]
        fixed = {order[stage]: value}
        for axis in order[stage + 1 :]:
            fixed[axis] = me.at[axis]
        return fixed

    sent = []
    pairs = ((x_ref, x_out), (g_ref, g_out))
    waits, arrivals, own_copies = [], [], []
    for piece in range(3):
        copy = pltpu.make_async_copy(
            blocks[piece], region(piece, around(piece, 0, me.at[GATHER_ORDERS[piece][0]])), local.at[piece]
        )
        copy.start()
        own_copies.append(copy)

    def semaphores(piece, stage, n, u):
        if stage == 2:
            return last_send.at[piece, u, n], last_recv.at[piece, u, n]
        return send.at[piece, stage, n], recv.at[piece, stage, n]

    def part(piece, stage, value, u, rows=None):
        fixed = around(piece, stage, value)
        if stage == 2:
            axis = GATHER_ORDERS[piece][1]
            fixed[axis] = lax.rem(me.at[axis] + (0, 3, 1, 2)[u], 4)
        return region(piece, fixed, rows)

    def begin(piece, stage, u=0):
        axis = GATHER_ORDERS[piece][stage]
        mine = part(piece, stage, me.at[axis], u)
        source = blocks[piece] if stage == 0 else mine
        for n, distance in enumerate((1, -1)):
            copy = remote(source, mine, *semaphores(piece, stage, n, u), me.step(axis, distance))
            copy.start()
            sent.append(copy)

    def arrived(piece, stage, n, u=0):
        axis = GATHER_ORDERS[piece][stage]
        value = lax.rem(me.at[axis] + (3, 1, 2, 2)[n], 4)
        there = part(piece, stage, value, u, (None, None, 0, 16)[n])
        remote(there, there, *semaphores(piece, stage, n, u), me.step(axis, 1)).wait_recv()
        if n < 2:
            half = part(piece, stage, value, u, (0, 16)[n])
            copy = remote(half, half, *semaphores(piece, stage, 2 + n, u), me.step(axis, (1, -1)[n]))
            copy.start()
            sent.append(copy)

    for piece in range(3):
        begin(piece, 0)
    partner, across = me.partner(), me.beside(2)

    def tokens_of(ref, col):
        return ref.at[:, pl.ds(pl.multiple_of(col // 2 * PAIR, PAIR), PAIR)]

    relays = []
    for n, (source, target) in enumerate(pairs + ((v_ref, v_out),)):
        here, there = (v_ref, v_ref) if n == 2 else (tokens_of(source, me.col), tokens_of(source, across[1]))
        own = pltpu.make_async_copy(here, target.at[me.col], in_local.at[n])
        own.start()
        waits.append(own)
        for k, (part_ref, device) in enumerate(((there, across), (here, partner))):
            copy = remote(part_ref, target.at[me.col], in_send.at[n, k], in_recv.at[n, k], device)
            copy.start()
            sent.append(copy)
        relays.append(remote(there, target.at[across[1]], in_send.at[n, 0], in_recv.at[n, 0], across))
        arrivals.append(remote(here, target.at[partner[1]], in_send.at[n, 1], in_recv.at[n, 1], partner))
    for copy in own_copies:
        copy.wait()
    for n in range(4):
        for piece in range(3):
            arrived(piece, 0, n)
    for piece in range(3):
        begin(piece, 1)
    for n, (_, target) in enumerate(pairs + ((v_ref, v_out),)):
        relays[n].wait_recv()
        block = target.at[across[1]]
        copy = remote(block, block, in_send.at[n, 2], in_recv.at[n, 2], partner)
        copy.start()
        sent.append(copy)
        far = target.at[lax.rem(partner[1] + 2, 4)]
        arrivals.append(remote(far, far, in_send.at[n, 2], in_recv.at[n, 2], partner))
    for piece in range(3):
        begin(piece, 2, 0)
    for n in range(4):
        for piece in range(3):
            arrived(piece, 1, n)
            if n < 2:
                begin(piece, 2, n + 1)
            elif n == 3:
                begin(piece, 2, 3)
    for n in (0, 1):
        for piece in range(3):
            arrived(piece, 2, n, 0)
    for u in range(1, 4):
        for n in (0, 1):
            for piece in range(3):
                arrived(piece, 2, n, u)
    for u in range(4):
        for n in (2, 3):
            for piece in range(3):
                arrived(piece, 2, n, u)
    for copy in arrivals:
        copy.wait_recv()
    for copy in waits:
        copy.wait()
    for copy in sent:
        copy.wait_send()


def gather_all(blocks, x, g, v):
    whole = jax.ShapeDtypeStruct((2, 2, 4, 4, 32, PACK), BF16)
    tokens = jax.ShapeDtypeStruct((4, 272, PAIR), BF16)
    return pl.pallas_call(
        gather_kernel,
        out_shape=(whole, whole, whole, tokens, tokens, jax.ShapeDtypeStruct((4, 8, 272), F32)),
        in_specs=[ANY] * 6,
        out_specs=(ANY,) * 6,
        scratch_shapes=[
            pltpu.SemaphoreType.DMA((3, 2, 4)),
            pltpu.SemaphoreType.DMA((3, 2, 4)),
            pltpu.SemaphoreType.DMA((3, 4, 4)),
            pltpu.SemaphoreType.DMA((3, 4, 4)),
            pltpu.SemaphoreType.DMA((3,)),
            pltpu.SemaphoreType.DMA((3, 3)),
            pltpu.SemaphoreType.DMA((3, 3)),
            pltpu.SemaphoreType.DMA((3,)),
        ],
        compiler_params=pltpu.CompilerParams(collective_id=0, has_side_effects=True),
        name="gather_weights",
    )(*blocks, x, g, v)


class Group:
    def __init__(self):
        self.row, self.col = lax.axis_index("row"), lax.axis_index("col")
        self.in_group = lax.rem(self.row + 2, 4)
        self.rank = self.in_group * 4 + self.col
        self.pair, self.core = self.rank // 2, lax.rem(self.col, 2)
        self.partner = (self.row, self.col + 1 - 2 * self.core)

    def device(self, other):
        return (lax.rem(self.row - self.in_group + other // 4 + 32, 32), lax.rem(other, 4))

    def greet(self):
        greet([self.device(lax.rem(self.rank + d, 16)) for d in range(1, 16)])

    def all_to_all(self, source, target, send, recv, local):
        own = pltpu.make_async_copy(source.at[self.rank], target.at[self.rank], local)
        own.start()
        sent, arrivals = [], []
        for d in range(1, 16):
            other = lax.rem(self.rank + d, 16)
            copy = remote(source.at[other], target.at[self.rank], send.at[d], recv.at[d], self.device(other))
            copy.start()
            sent.append(copy)
            origin = lax.rem(self.rank + 16 - d, 16)
            arrivals.append(remote(source.at[other], target.at[origin], send.at[d], recv.at[d], self.device(origin)))
        return own, sent, arrivals

    def finish(self, own, sent, arrivals):
        for copy in arrivals:
            copy.wait_recv()
        for copy in sent:
            copy.wait_send()
        own.wait()

    def relay(self, source_of, target, send, recv, local):
        own = pltpu.make_async_copy(source_of(self.pair), target.at[self.rank], local)
        own.start()
        beside = remote(source_of(self.pair), target.at[self.rank], send.at[0, 0], recv.at[0, 0], self.partner)
        beside.start()
        sent = [beside]
        for e in range(1, 8):
            other = lax.rem(self.pair + e, 8)
            copy = remote(
                source_of(other), target.at[self.rank], send.at[0, e], recv.at[0, e], self.device(other * 2 + self.core)
            )
            copy.start()
            sent.append(copy)
        return own, sent

    def pass_on(self, own, sent, target, send, recv):
        for e in range(1, 8):
            origin = lax.rem(self.pair + 8 - e, 8) * 2 + self.core
            block = target.at[origin]
            remote(block, block, send.at[0, e], recv.at[0, e], self.device(origin)).wait_recv()
            copy = remote(block, block, send.at[1, e], recv.at[1, e], self.partner)
            copy.start()
            sent.append(copy)
        for e in range(0, 8):
            block = target.at[lax.rem(self.pair + 8 - e, 8) * 2 + 1 - self.core]
            n = 0 if e == 0 else 1
            remote(block, block, send.at[n, e], recv.at[n, e], self.partner).wait_recv()
        for copy in sent:
            copy.wait_send()
        own.wait()


RELAY = [pltpu.SemaphoreType.DMA((2, 8)), pltpu.SemaphoreType.DMA((2, 8)), pltpu.SemaphoreType.DMA]
DIRECT = [pltpu.SemaphoreType.DMA((16,)), pltpu.SemaphoreType.DMA((16,)), pltpu.SemaphoreType.DMA]


def exchange_call(kernel, name, collective_id, outs, scratch, *args, in_specs=None):
    return pl.pallas_call(
        kernel,
        out_shape=outs,
        in_specs=in_specs or [ANY] * len(args),
        out_specs=(ANY,) * len(outs),
        scratch_shapes=scratch,
        compiler_params=pltpu.CompilerParams(collective_id=collective_id, has_side_effects=True),
        name=name,
    )(*args)


def qkv_exchange_kernel(source, last, target, last_out, send, recv, local, rsend, rrecv, rlocal):
    group = Group()
    group.greet()
    relayed = group.relay(lambda p: last, last_out, rsend, rrecv, rlocal)
    direct = group.all_to_all(source, target, send, recv, local)
    group.pass_on(*relayed, last_out, rsend, rrecv)
    group.finish(*direct)


def qkv_exchange(source, last):
    outs = (jax.ShapeDtypeStruct((16, 192, 128), BF16), jax.ShapeDtypeStruct((16, QUARTER, 128), BF16))
    return exchange_call(qkv_exchange_kernel, "exchange_qkv", 1, outs, DIRECT + RELAY, source, last)


def mixed_exchange_kernel(source, last, target, last_out, send, recv, local, last_send, last_recv, last_local):
    group = Group()
    group.greet()
    relayed = group.relay(lambda p: source.at[p], target, send, recv, local)
    own = pltpu.make_async_copy(last, last_out.at[group.core], last_local)
    own.start()
    copy = remote(last, last_out.at[group.core], last_send, last_recv, group.partner)
    copy.start()
    group.pass_on(*relayed, target, send, recv)
    remote(last, last_out.at[1 - group.core], last_send, last_recv, group.partner).wait_recv()
    copy.wait_send()
    own.wait()


def mixed_exchange(source, last):
    outs = (jax.ShapeDtypeStruct((16, 128, 128), BF16), jax.ShapeDtypeStruct((2, QUARTER, 64), BF16))
    return exchange_call(
        mixed_exchange_kernel, "exchange_mixed", 2, outs, RELAY + [pltpu.SemaphoreType.DMA] * 3, source, last
    )


def grad_exchange_kernel(source, target, send, recv, local):
    group = Group()
    group.greet()
    group.finish(*group.all_to_all(source, target, send, recv, local))


def grad_exchange(source):
    outs = (jax.ShapeDtypeStruct((16, 64, 128), BF16),)
    return exchange_call(grad_exchange_kernel, "exchange_d_mix", 7, outs, DIRECT, source)[0]


def back_exchange_kernel(
    source, parts, target, sums_out, send, recv, local, theirs, summed, swap_send, swap_recv, psend, precv, plocal
):
    group = Group()
    group.greet()
    swap = remote(parts.at[:, 1 - group.core], theirs, swap_send, swap_recv, group.partner)
    swap.start()
    direct = group.all_to_all(source, target, send, recv, local)
    swap.wait_recv()

    @pl.loop(0, 8)
    def _(p):
        summed[p] = (parts[p, group.core].astype(F32) + theirs[p].astype(F32)).astype(BF16)

    own = pltpu.make_async_copy(summed.at[group.pair], sums_out.at[group.pair], plocal)
    own.start()
    sent = [swap]
    for e in range(1, 8):
        other = lax.rem(group.pair + e, 8)
        copy = remote(
            summed.at[other], sums_out.at[group.pair], psend.at[e], precv.at[e], group.device(other * 2 + group.core)
        )
        copy.start()
        sent.append(copy)
    for e in range(1, 8):
        origin = lax.rem(group.pair + 8 - e, 8)
        block = sums_out.at[origin]
        remote(block, block, psend.at[e], precv.at[e], group.device(origin * 2 + group.core)).wait_recv()
    group.finish(*direct)
    for copy in sent:
        copy.wait_send()
    own.wait()


def back_exchange(source, parts):
    outs = (jax.ShapeDtypeStruct((16, 192, 128), BF16), jax.ShapeDtypeStruct((8, QUARTER, 128), BF16))
    block = pltpu.VMEM((8, QUARTER, 128), BF16)
    scratch = DIRECT + [block, block, pltpu.SemaphoreType.DMA, pltpu.SemaphoreType.DMA] + [
        pltpu.SemaphoreType.DMA((8,)), pltpu.SemaphoreType.DMA((8,)), pltpu.SemaphoreType.DMA
    ]
    return exchange_call(
        back_exchange_kernel, "exchange_d_qkv", 8, outs, scratch, source, parts, in_specs=[ANY, VMEM_SPEC]
    )


def free_axes(fixed):
    return [axis for axis in ("y", "z", "x") if axis not in fixed]


def buffer_shape(fixed, rows):
    shape = ()
    for axis in free_axes(fixed):
        shape = shape + ((2, 2) if axis == "y" else (4,))
    return shape + (rows, PACK)


def buffer_index(at):
    index = ()
    for axis in ("y", "z", "x"):
        if axis in at:
            index = index + ((lax.rem(at[axis], 2), at[axis] // 2) if axis == "y" else (at[axis],))
    return index


VECTOR_AXES = ("z", "x", "y")


def scatter_kernel(part0, part1, part2, y_ref, gin_ref, v_ref, out_ref, y_out, gin_out, v_out, *scratch):
    me = Place()
    parts = (part0, part1, part2)
    sums = scratch[0:3]
    halves = {}
    fulls = {}
    position = 3
    for piece in range(3):
        for stage in range(3):
            halves[piece, stage] = scratch[position : position + 2]
            fulls[piece, stage] = scratch[position + 2 : position + 4]
            position += 4
    vectors = scratch[position : position + 3]
    position += 3
    local, big_send, big_recv, send, recv, out_send, out_recv, out_local, v_send, v_recv = scratch[position:]
    greet(me.neighbours() + [me.step(axis, 2) for axis in VECTOR_AXES])

    sent, loads = [], {}
    for k in range(3):
        for u in range(4):
            for piece in range(3):
                first, second = SCATTER_ORDERS[piece][:2]
                index = place_index(
                    {first: lax.rem(me.at[first] + (2, 1, 3)[k], 4), second: lax.rem(me.at[second] + (2, 1, 3, 0)[u], 4)}
                )
                load = pltpu.make_async_copy(parts[piece].at[index], sums[piece].at[index], local.at[piece, k, u])
                load.start()
                loads[piece, k, u] = load
    for u in range(4):
        for piece in range(3):
            first, second = SCATTER_ORDERS[piece][:2]
            index = place_index({first: me.at[first], second: lax.rem(me.at[second] + (2, 1, 3, 0)[u], 4)})
            load = pltpu.make_async_copy(parts[piece].at[index], sums[piece].at[index], local.at[piece, 3, u])
            load.start()
            loads[piece, 3, u] = load

    def vectors_begin(phase, value):
        axis = VECTOR_AXES[phase]
        mine = vectors[phase].at[me.at[axis]]
        mine[...] = value
        for distance in (1, 2, 3):
            copy = remote(
                mine, mine, v_send.at[phase, distance - 1], v_recv.at[phase, distance - 1], me.step(axis, distance)
            )
            copy.start()
            sent.append(copy)

    def vectors_end(phase):
        axis = VECTOR_AXES[phase]
        for distance in (1, 2, 3):
            there = vectors[phase].at[lax.rem(me.at[axis] + 4 - distance, 4)]
            remote(
                there, there, v_send.at[phase, distance - 1], v_recv.at[phase, distance - 1], me.step(axis, distance)
            ).wait_recv()
        buffer = vectors[phase]
        return (buffer[0] + buffer[1]) + (buffer[2] + buffer[3])

    def stage_fixed(piece, stage):
        return {axis: me.at[axis] for axis in SCATTER_ORDERS[piece][:stage]}

    def each_tile(fixed, body):
        axes = free_axes(fixed)
        count = 4 ** len(axes)
        if count == 1:
            body({})
            return

        @pl.loop(0, count)
        def _(t):
            if len(axes) == 1:
                body({axes[0]: t})
            else:
                body({axes[0]: t // 4, axes[1]: lax.rem(t, 4)})

    def chunk(piece, stage, u):
        if stage > 0:
            return {}
        axis = SCATTER_ORDERS[piece][1]
        return {axis: lax.rem(me.at[axis] + (2, 1, 3, 0)[u], 4)}

    def sems(piece, stage, n, u):
        if stage == 0:
            return big_send.at[piece, u, n], big_recv.at[piece, u, n]
        return send.at[piece, stage - 1, n], recv.at[piece, stage - 1, n]

    def part_of(buffer, piece, stage, u):
        if stage > 0:
            return buffer
        axis = SCATTER_ORDERS[piece][1]
        value = lax.rem(me.at[axis] + (2, 1, 3, 0)[u], 4)
        index = ()
        for name in free_axes({SCATTER_ORDERS[piece][0]: 0}):
            if name == "y":
                index += (lax.rem(value, 2), value // 2) if name == axis else (everything(), everything())
            else:
                index += (value,) if name == axis else (everything(),)
        return buffer.at[index]

    def begin(piece, stage, u=0):
        axis = SCATTER_ORDERS[piece][stage]
        fixed = {**stage_fixed(piece, stage), axis: lax.rem(me.at[axis] + 2, 4), **chunk(piece, stage, u)}
        for n in range(2):
            copy = remote(
                sums[piece].at[place_index(fixed) + (pl.ds(16 * n, 16),)],
                part_of(halves[piece, stage][n], piece, stage, u),
                *sems(piece, stage, n, u), me.step(axis, (1, -1)[n]),
            )
            copy.start()
            sent.append(copy)

    def middle(piece, stage, n, u=0):
        axis = SCATTER_ORDERS[piece][stage]
        more = chunk(piece, stage, u)
        fixed = {**stage_fixed(piece, stage), axis: lax.rem(me.at[axis] + (1, 3)[n], 4), **more}
        half = halves[piece, stage][n]
        there = part_of(half, piece, stage, u)
        remote(there, there, *sems(piece, stage, n, u), me.step(axis, 1)).wait_recv()

        def body(at):
            index = place_index({**fixed, **at}) + (pl.ds(16 * n, 16),)
            total = sums[piece][index].astype(F32) + half[buffer_index({**more, **at})].astype(F32)
            sums[piece][index] = total.astype(BF16)

        each_tile(fixed, body)
        copy = remote(
            sums[piece].at[place_index(fixed)], part_of(fulls[piece, stage][n], piece, stage, u),
            *sems(piece, stage, 2 + n, u), me.step(axis, (1, -1)[n]),
        )
        copy.start()
        sent.append(copy)

    def finish(piece, stage, u=0):
        axis = SCATTER_ORDERS[piece][stage]
        more = chunk(piece, stage, u)
        fixed = {**stage_fixed(piece, stage), axis: me.at[axis], **more}
        first, second = fulls[piece, stage]
        for n, buffer in enumerate((first, second)):
            there = part_of(buffer, piece, stage, u)
            remote(there, there, *sems(piece, stage, 2 + n, u), me.step(axis, 1)).wait_recv()

        def body(at):
            index = place_index({**fixed, **at})
            place = buffer_index({**more, **at})
            if stage == 2:
                total = sums[piece][index].astype(F32) + (first[...].astype(F32) + second[...].astype(F32))
                out_ref[piece] = total
            else:
                total = sums[piece][index].astype(F32) + (first[place].astype(F32) + second[place].astype(F32))
                sums[piece][index] = total.astype(BF16)

        each_tile(fixed, body)

    for u in range(4):
        for piece in range(3):
            loads[piece, 0, u].wait()
            begin(piece, 0, u)
    vectors_begin(0, v_ref[...])

    pairs = ((y_ref, y_out), (gin_ref, gin_out))
    arrivals, own_copies = [], []
    for n, (source, target) in enumerate(pairs):
        rows = pl.ds(pl.multiple_of(me.col * QUARTER, QUARTER), QUARTER)
        own = pltpu.make_async_copy(source.at[me.col], target.at[:, rows], out_local.at[n])
        own.start()
        own_copies.append(own)
        for distance in (1, 2, 3):
            peer = me.beside(distance)
            semaphore = (out_send.at[n, distance - 1], out_recv.at[n, distance - 1])
            copy = remote(source.at[peer[1]], target.at[:, rows], *semaphore, peer)
            copy.start()
            sent.append(copy)
            origin = pl.ds(pl.multiple_of(lax.rem(me.col + 4 - distance, 4) * QUARTER, QUARTER), QUARTER)
            arrivals.append(remote(source.at[me.col], target.at[:, origin], *semaphore, peer))

    def finish_chunk(u):
        for piece in range(3):
            loads[piece, 3, u].wait()
            finish(piece, 0, u)
            if u == 0:
                begin(piece, 1)
            elif u < 3:
                middle(piece, 1, u - 1)
            else:
                finish(piece, 1)
                begin(piece, 2)

    for u in range(4):
        for n in range(2):
            for piece in range(3):
                loads[piece, 1 + n, u].wait()
                middle(piece, 0, n, u)
        if u < 2:
            vectors_begin(u + 1, vectors_end(u))
        if u == 3:
            v_out[...] = vectors_end(2)
        if u > 0:
            finish_chunk(u - 1)
    finish_chunk(3)
    for n in range(2):
        for piece in range(3):
            middle(piece, 2, n)
    for piece in range(3):
        finish(piece, 2)
    for copy in arrivals:
        copy.wait_recv()
    for copy in own_copies:
        copy.wait()
    for copy in sent:
        copy.wait_send()


def scatter_all(parts, y4, gin4, vectors):
    scratch = [pltpu.VMEM((2, 2, 4, 4, 32, PACK), BF16) for _ in range(3)]
    for piece in range(3):
        order = SCATTER_ORDERS[piece]
        for stage in range(3):
            fixed = order[: stage + 1]
            scratch += [pltpu.VMEM(buffer_shape(fixed, 16), BF16) for _ in range(2)]
            scratch += [pltpu.VMEM(buffer_shape(fixed, 32), BF16) for _ in range(2)]
    scratch += [pltpu.VMEM((4, 8, WIDE), F32) for _ in range(3)]
    scratch += [
        pltpu.SemaphoreType.DMA((3, 4, 4)),
        pltpu.SemaphoreType.DMA((3, 4, 4)),
        pltpu.SemaphoreType.DMA((3, 4, 4)),
        pltpu.SemaphoreType.DMA((3, 2, 4)),
        pltpu.SemaphoreType.DMA((3, 2, 4)),
        pltpu.SemaphoreType.DMA((2, 3)),
        pltpu.SemaphoreType.DMA((2, 3)),
        pltpu.SemaphoreType.DMA((2,)),
        pltpu.SemaphoreType.DMA((3, 3)),
        pltpu.SemaphoreType.DMA((3, 3)),
    ]
    back = jax.ShapeDtypeStruct((272, 512), BF16)
    return pl.pallas_call(
        scatter_kernel,
        out_shape=(jax.ShapeDtypeStruct((3, 32, PACK), F32), back, back, jax.ShapeDtypeStruct((8, WIDE), F32)),
        in_specs=[ANY] * 5 + [VMEM_SPEC],
        out_specs=(VMEM_SPEC, ANY, ANY, VMEM_SPEC),
        scratch_shapes=scratch,
        compiler_params=pltpu.CompilerParams(
            collective_id=3, has_side_effects=True, vmem_limit_bytes=VMEM_LIMIT
        ),
        name="scatter_gradients",
    )(*parts, y4, gin4, vectors)


def unpack_tail(packed, tiles, wide, tail):
    tiles[...] = packed[:, WIDE:PACK].astype(F32)
    for j in range(2):
        for s in range(9):
            wide[pl.ds(32 * j, 32), pl.ds(128 * s, 128)] = tiles[pl.ds(9 * j + s, 32, stride=32), :]
    tail[0:64, :] = wide[0:64, :].astype(BF16)


def pack_tail(tail, tiles, packed):
    for j in range(2):
        for s in range(9):
            tiles[pl.ds(9 * j + s, 32, stride=32), :] = tail[32 * j : 32 * j + 32, 128 * s : 128 * s + 128]
    packed[:, WIDE:PACK] = tiles[...].astype(BF16)


def in_features(values, packed, tail, columns):
    return dot_nn(values[:, :MAIN], packed[:, columns]) + dot_nn(values[:, MAIN:], tail[:, columns])


def add_to_features(total_t, values_t, packed, tail):
    @pl.loop(0, 4)
    def _(b):
        rows = pl.ds(pl.multiple_of(b * 256, 256), 256)
        total_t[rows, :] += dot_nn(packed[rows, :WIDE], values_t[...])

    total_t[MAIN:, :] += dot_nn(tail[...], values_t[...])


def norm_forward(x, gain, bias):
    mean = jnp.sum(x, axis=1, keepdims=True) / D
    square = jnp.sum(x * x, axis=1, keepdims=True) / D
    inverse = lax.rsqrt(square - mean * mean + norm_epsilon)
    normed = (x - mean) * inverse
    return normed, inverse, (normed * gain + bias).astype(BF16)


def norm_reverse(grad, normed, inverse, gain):
    scaled = grad * gain
    first = jnp.sum(scaled, axis=1, keepdims=True) / D
    second = jnp.sum(scaled * normed, axis=1, keepdims=True) / D
    return inverse * (scaled - first - normed * second)


def permuted(pieces, perm):
    total = dot_nn(pieces[0].astype(F32).T.astype(BF16), perm[0])
    for c in range(1, 4):
        total += dot_nn(pieces[c].astype(F32).T.astype(BF16), perm[c])
    return total


def permuted_exact(pieces, perm):
    total = jnp.zeros((8, WIDE), F32)
    for c in range(4):
        left = pieces[c]
        for _ in range(3):
            part = left.astype(BF16)
            left = left - part.astype(F32)
            total += dot_nn(part, perm[c])
    return total


def real_features(values):
    lane = lax.broadcasted_iota(jnp.int32, values.shape, 1)
    return jnp.where(lane < D, values, 0.0)


def turned(values):
    return values.astype(F32).T.astype(BF16)


def own_half(core):
    return pl.ds(pl.multiple_of(core * QUARTER, QUARTER), QUARTER)


def load_weights(source, target, semaphores):
    copies = []
    for j in range(2):
        copy = pltpu.make_async_copy(source.at[j], target.at[j], semaphores.at[j])
        copy.start()
        copies.append(copy)
    return copies


def qkv_kernel(
    x4, v4, perm, w_ref, x_out, n1_out, v_out, msg, last, q16, w, qkv, qkv_out, tiles, wide, tail, load, send, recv, local
):
    me = Place()
    partner = me.partner()
    copies = load_weights(w_ref, w, load)
    greet([partner])
    x = permuted(x4, perm)
    vectors = permuted_exact(v4, perm)
    v_out[...] = vectors
    x_out[...] = x.astype(BF16)
    _, _, normed = norm_forward(x, vectors[0:1], vectors[1:2])
    n1_out[...] = normed
    tail[...] = jnp.zeros_like(tail)
    mine, theirs = own_half(me.core), own_half(1 - me.core)
    sent, own_copies, arrivals = [], [], []
    for j in range(2):
        copies[j].wait()
        packed = w.at[j]
        unpack_tail(packed, tiles, wide, tail)

        @pl.loop(0, 3)
        def _(b):
            columns = pl.ds(pl.multiple_of(b * 384, 128), 384)
            qkv[j, :, columns] = in_features(n1_out[...], packed, tail, columns).astype(BF16)

        own = pltpu.make_async_copy(qkv.at[j, mine, :], qkv_out.at[j, me.core], local.at[j])
        own.start()
        own_copies.append(own)
        copy = remote(qkv.at[j, theirs, :], qkv_out.at[j, me.core], send.at[j], recv.at[j], partner)
        copy.start()
        sent.append(copy)
        arrivals.append(
            remote(qkv.at[j, theirs, :], qkv_out.at[j, 1 - me.core], send.at[j], recv.at[j], partner)
        )
    for copy in arrivals:
        copy.wait_recv()
    for copy in own_copies:
        copy.wait()
    for n in range(3):
        for head in range(HEADS):
            block = columns_of(qkv_out, n * D + head * HEAD_DIM, QKV_COLS, 0)
            if head == 16:
                if n == 0:
                    q16[...] = block
                else:
                    last[:, 64 * (n - 1) : 64 * n] = block
            else:
                msg[head, 64 * n : 64 * n + 64, 0:64] = block[0:64]
                msg[head, 64 * n : 64 * n + 64, 64:128] = block[64:128]
    for copy in sent:
        copy.wait_send()


def columns_of(blocks, start, width, offset):
    pieces = []
    position = start
    while position < start + HEAD_DIM:
        c = position // width
        end = min(start + HEAD_DIM, (c + 1) * width)
        first = position - c * width + offset
        pieces.append(blocks[c // 2, c % 2, :, first : first + end - position])
        position = end
    return pieces[0] if len(pieces) == 1 else jnp.concatenate(pieces, axis=1)


def qkv_call(x4, v4, perm, weights):
    row = jax.ShapeDtypeStruct((PAIR, WIDE), BF16)
    return pl.pallas_call(
        qkv_kernel,
        out_shape=(
            row, row, jax.ShapeDtypeStruct((8, WIDE), F32), jax.ShapeDtypeStruct((16, 192, 128), BF16),
            jax.ShapeDtypeStruct((QUARTER, 128), BF16), jax.ShapeDtypeStruct((QUARTER, 64), BF16),
        ),
        in_specs=[VMEM_SPEC, VMEM_SPEC, VMEM_SPEC, ANY],
        out_specs=(VMEM_SPEC,) * 6,
        scratch_shapes=[
            pltpu.VMEM((2, MAIN, PACK), BF16), pltpu.VMEM((2, PAIR, WIDE), BF16),
            pltpu.VMEM((2, 2, QUARTER, WIDE), BF16),
            pltpu.VMEM((MAIN, 128), F32), pltpu.VMEM((128, WIDE), F32), pltpu.VMEM((128, WIDE), BF16),
            pltpu.SemaphoreType.DMA((2,)), pltpu.SemaphoreType.DMA((2,)), pltpu.SemaphoreType.DMA((2,)),
            pltpu.SemaphoreType.DMA((2,)),
        ],
        compiler_params=pltpu.CompilerParams(
            collective_id=4, has_side_effects=True, vmem_limit_bytes=VMEM_LIMIT
        ),
        name="norm_and_qkv",
    )(x4, v4, perm, weights)


def gelu_both(v):
    square = v * v
    tanh_value = jnp.tanh(gelu_coef * (v + 0.044715 * v * square))
    half = 0.5 * (1.0 + tanh_value)
    value = v * half
    slope = half + 0.5 * v * (1.0 - tanh_value * tanh_value) * gelu_coef * (1.0 + 0.134145 * square)
    return value, slope


def weight_gradient(rows_t, values, tiles, tail_sum, packed):
    @pl.loop(0, 4)
    def _(b):
        rows = pl.ds(pl.multiple_of(b * 256, 256), 256)
        packed[rows, :WIDE] = dot_nn(rows_t[rows, :], values[...]).astype(BF16)

    tail_sum[...] = dot_nn(rows_t[MAIN:, :], values[...])
    pack_tail(tail_sum, tiles, packed)


def swap_start(total_t, mine, theirs, ssem, rsem, partner):
    mine[...] = total_t[...].astype(BF16)
    copy = remote(mine, theirs, ssem, rsem, partner)
    copy.start()
    return copy


def swap_end(copy, mine, theirs):
    copy.wait_recv()
    return mine[...].astype(F32) + theirs[...].astype(F32)


def middle_kernel(
    x_ref, a0, w0_ref, w1_ref, w2_ref, g4, perm, vec,
    y4, dres_out, dresb_out, gr1_out, gr2_out, dmsg, dlast, vec_out,
    w0, w1, w2, gr1, gr2, resid, normed2, inverse2, n2, n2_t, cot, cot_t, total_t, dn2_t, hidden, dpre, turn1, turn2,
    dmix, tiles, out_tiles, tail1, tail2, tail_sum, mine1, theirs1, mine2, theirs2, mine_y, theirs_y, dmix_out,
    load, store, send, recv, local,
):
    me = Place()
    partner = me.partner()
    loads = [load_weights(source, target, load.at[n]) for n, (source, target) in enumerate(
        ((w0_ref, w0), (w1_ref, w1), (w2_ref, w2))
    )]
    greet([partner])
    for buffer in (tail1, tail2, out_tiles, total_t, dn2_t):
        buffer[...] = jnp.zeros_like(buffer)
    for j in range(2):
        turn1[...] = turned(a0[j])
        loads[0][j].wait()
        unpack_tail(w0.at[j], tiles, tail_sum, tail1)
        add_to_features(total_t, turn1, w0.at[j], tail1)
    first = swap_start(total_t, mine1, theirs1, send.at[0], recv.at[0], partner)
    cot_value = permuted(g4, perm)
    cot[...] = cot_value.astype(BF16)
    cot_t[...] = cot_value.T.astype(BF16)
    total_t[...] = jnp.zeros_like(total_t)
    attended = swap_end(first, mine1, theirs1)
    resid[...] = x_ref[...].astype(F32) + attended.T
    normed, inverse, n2_value = norm_forward(resid[...], vec[2:3], vec[3:4])
    normed2[...] = normed
    inverse2[...] = jnp.broadcast_to(inverse, inverse2.shape)
    n2[...] = n2_value
    n2_t[...] = turned(n2_value)
    stores = []
    for j in range(2):
        loads[1][j].wait()
        loads[2][j].wait()
        up, down = w1.at[j], w2.at[j]
        unpack_tail(up, tiles, tail_sum, tail1)
        unpack_tail(down, tiles, tail_sum, tail2)

        @pl.loop(0, 3)
        def _(b):
            columns = pl.ds(pl.multiple_of(b * 384, 128), 384)
            pre = in_features(n2[...], up, tail1, columns)
            d_hidden = in_features(cot[...], down, tail2, columns)
            value, slope = gelu_both(pre)
            hidden[:, columns] = value.astype(BF16)
            dpre[:, columns] = (d_hidden * slope).astype(BF16)

        turn1[...] = turned(hidden[...])
        turn2[...] = turned(dpre[...])
        add_to_features(total_t, turn1, down, tail2)
        add_to_features(dn2_t, turn2, up, tail1)
        if j == 1:
            second = swap_start(dn2_t, mine2, theirs2, send.at[1], recv.at[1], partner)
            half = own_half(1 - me.core)
            mine_y[...] = total_t[:, half].astype(BF16)
            third = remote(mine_y, theirs_y, send.at[2], recv.at[2], partner)
            third.start()
        weight_gradient(n2_t, dpre, out_tiles, tail_sum, gr1.at[j])
        weight_gradient(cot_t, hidden, out_tiles, tail_sum, gr2.at[j])
        for n, (source, target) in enumerate(((gr1, gr1_out), (gr2, gr2_out))):
            copy = pltpu.make_async_copy(source.at[j], target.at[j], store.at[n, j])
            copy.start()
            stores.append(copy)
    grad = swap_end(second, mine2, theirs2).T
    normed = normed2[...]
    vec_out[...] = jnp.zeros_like(vec_out)
    vec_out[0:1, :] = jnp.sum(grad * normed, axis=0, keepdims=True)
    vec_out[1:2, :] = jnp.sum(grad, axis=0, keepdims=True)
    back = cot[...].astype(F32) + norm_reverse(grad, normed, inverse2[:, 0:1], vec[2:3])
    back = real_features(back)
    dres_out[...] = back
    dresb_out[...] = back.astype(BF16)
    sent, own_copies, arrivals = [first, second, third], [], []
    columns = slice(768, WIDE)
    for j in range(2):
        unpack_tail(w0.at[j], tiles, tail_sum, tail1)
        dmix[j] = in_features(dresb_out[...], w0.at[j], tail1, columns).astype(BF16)
        own = pltpu.make_async_copy(dmix.at[j, own_half(me.core), :], dmix_out.at[j, me.core], local.at[j])
        own.start()
        own_copies.append(own)
        theirs = dmix.at[j, own_half(1 - me.core), :]
        copy = remote(theirs, dmix_out.at[j, me.core], send.at[3 + j], recv.at[3 + j], partner)
        copy.start()
        sent.append(copy)
        arrivals.append(remote(theirs, dmix_out.at[j, 1 - me.core], send.at[3 + j], recv.at[3 + j], partner))
    half = own_half(me.core)
    third.wait_recv()
    y = (resid[half, :].T + (total_t[:, half] + theirs_y[...].astype(F32))).astype(BF16)
    for c in range(4):
        y4[c] = dot_nn(perm[c], y).astype(BF16)
    for copy in arrivals:
        copy.wait_recv()
    for copy in own_copies:
        copy.wait()
    for head in range(HEADS):
        block = columns_of(dmix_out, head * HEAD_DIM, 272, QKV_COLS - 768)
        if head == 16:
            dlast[...] = block
        else:
            dmsg[head, :, 0:64] = block[0:64]
            dmsg[head, :, 64:128] = block[64:128]
    for copy in stores:
        copy.wait()
    for copy in sent:
        copy.wait_send()


def middle_call(x, a0, w0, w1, w2, g4, perm, vec):
    packed = jax.ShapeDtypeStruct((2, MAIN, PACK), BF16)
    weights = pltpu.VMEM((2, MAIN, PACK), BF16)
    row_f, row_b = pltpu.VMEM((PAIR, WIDE), F32), pltpu.VMEM((PAIR, WIDE), BF16)
    turn_f, turn_b = pltpu.VMEM((WIDE, PAIR), F32), pltpu.VMEM((WIDE, PAIR), BF16)
    tile, tail = pltpu.VMEM((MAIN, 128), F32), pltpu.VMEM((128, WIDE), BF16)
    half = pltpu.VMEM((WIDE, QUARTER), BF16)
    return pl.pallas_call(
        middle_kernel,
        out_shape=(
            jax.ShapeDtypeStruct((4, 272, QUARTER), BF16), jax.ShapeDtypeStruct((PAIR, WIDE), F32),
            jax.ShapeDtypeStruct((PAIR, WIDE), BF16), packed, packed,
            jax.ShapeDtypeStruct((16, 64, 128), BF16), jax.ShapeDtypeStruct((QUARTER, 64), BF16),
            jax.ShapeDtypeStruct((8, WIDE), F32),
        ),
        in_specs=[VMEM_SPEC, VMEM_SPEC, ANY, ANY, ANY, VMEM_SPEC, VMEM_SPEC, VMEM_SPEC],
        out_specs=(VMEM_SPEC, VMEM_SPEC, VMEM_SPEC, ANY, ANY, VMEM_SPEC, VMEM_SPEC, VMEM_SPEC),
        scratch_shapes=[
            weights, weights, weights, weights, weights, row_f, row_f, pltpu.VMEM((PAIR, 128), F32), row_b, turn_b,
            row_b, turn_b, turn_f, turn_f, row_b, row_b, turn_b, turn_b, pltpu.VMEM((2, PAIR, 384), BF16),
            tile, tile, tail, tail, pltpu.VMEM((128, WIDE), F32), turn_b, turn_b, turn_b, turn_b, half, half,
            pltpu.VMEM((2, 2, QUARTER, 384), BF16),
            pltpu.SemaphoreType.DMA((3, 2)), pltpu.SemaphoreType.DMA((2, 2)), pltpu.SemaphoreType.DMA((5,)),
            pltpu.SemaphoreType.DMA((5,)), pltpu.SemaphoreType.DMA((2,)),
        ],
        compiler_params=pltpu.CompilerParams(
            collective_id=5, has_side_effects=True, vmem_limit_bytes=VMEM_LIMIT
        ),
        name="feed_forward",
    )(x, a0, w0, w1, w2, g4, perm, vec)


def first_kernel(
    x_ref, n1, dresb, dres, dq_ref, a0, w0_ref, perm, vec, vec2,
    gin4, gr0_out, sums,
    w0, gr0, dq, n1_t, dres_t, turn, dn1_t, tiles, out_tiles, tail, tail_sum, mine, theirs,
    load, store, send, recv, local,
):
    me = Place()
    partner = me.partner()
    loads = load_weights(w0_ref, w0, load)
    greet([partner])
    mine_rows = own_half(me.core)
    copy = remote(dq_ref.at[1 - me.core], dq.at[:, mine_rows, :], send.at[0], recv.at[0], partner)
    copy.start()
    own = pltpu.make_async_copy(dq_ref.at[me.core], dq.at[:, mine_rows, :], local)
    own.start()
    for buffer in (tail, out_tiles, dn1_t):
        buffer[...] = jnp.zeros_like(buffer)
    n1_t[...] = turned(n1[...])
    dres_t[...] = turned(dresb[...])
    normed, inverse, _ = norm_forward(x_ref[...].astype(F32), vec[0:1], vec[1:2])
    own.wait()
    remote(
        dq_ref.at[me.core], dq.at[:, own_half(1 - me.core), :], send.at[0], recv.at[0], partner
    ).wait_recv()
    for j in range(2):
        loads[j].wait()
        unpack_tail(w0.at[j], tiles, tail_sum, tail)
        turn[...] = turned(dq[j])
        add_to_features(dn1_t, turn, w0.at[j], tail)
    swap = swap_start(dn1_t, mine, theirs, send.at[1], recv.at[1], partner)
    stores = []
    for j in range(2):
        packed = gr0.at[j]

        @pl.loop(0, 4)
        def _(b):
            rows = pl.ds(pl.multiple_of(b * 256, 256), 256)
            packed[rows, :768] = dot_nn(n1_t[rows, :], dq[j, :, :768]).astype(BF16)
            packed[rows, 768:WIDE] = (
                dot_nn(n1_t[rows, :], dq[j, :, 768:]) + dot_nn(dres_t[rows, :], a0[j, :, 768:])
            ).astype(BF16)

        tail_sum[:, :768] = dot_nn(n1_t[MAIN:, :], dq[j, :, :768])
        tail_sum[:, 768:] = dot_nn(n1_t[MAIN:, :], dq[j, :, 768:]) + dot_nn(dres_t[MAIN:, :], a0[j, :, 768:])
        pack_tail(tail_sum, out_tiles, packed)
        out = pltpu.make_async_copy(packed, gr0_out.at[j], store.at[j])
        out.start()
        stores.append(out)
    grad = swap_end(swap, mine, theirs).T
    sums[...] = vec2[...]
    sums[4:5, :] = jnp.sum(grad * normed, axis=0, keepdims=True)
    sums[5:6, :] = jnp.sum(grad, axis=0, keepdims=True)
    back = dres[...] + norm_reverse(grad, normed, inverse, vec[0:1])
    dn1_t[...] = real_features(back).T
    back = dn1_t[:, mine_rows].astype(BF16)
    for c in range(4):
        gin4[c] = dot_nn(perm[c], back).astype(BF16)
    for out in stores:
        out.wait()
    copy.wait_send()
    swap.wait_send()


def first_call(x, n1, dresb, dres, dq, a0, w0, perm, vec, vec2):
    weights = pltpu.VMEM((2, MAIN, PACK), BF16)
    turn_b = pltpu.VMEM((WIDE, PAIR), BF16)
    tile = pltpu.VMEM((MAIN, 128), F32)
    return pl.pallas_call(
        first_kernel,
        out_shape=(
            jax.ShapeDtypeStruct((4, 272, QUARTER), BF16), jax.ShapeDtypeStruct((2, MAIN, PACK), BF16),
            jax.ShapeDtypeStruct((8, WIDE), F32),
        ),
        in_specs=[VMEM_SPEC] * 4 + [ANY, VMEM_SPEC, ANY] + [VMEM_SPEC] * 3,
        out_specs=(VMEM_SPEC, ANY, VMEM_SPEC),
        scratch_shapes=[
            weights, weights, pltpu.VMEM((2, PAIR, WIDE), BF16), turn_b, turn_b, turn_b,
            pltpu.VMEM((WIDE, PAIR), F32), tile, tile, pltpu.VMEM((128, WIDE), BF16), pltpu.VMEM((128, WIDE), F32),
            turn_b, turn_b,
            pltpu.SemaphoreType.DMA((2,)), pltpu.SemaphoreType.DMA((2,)), pltpu.SemaphoreType.DMA((2,)),
            pltpu.SemaphoreType.DMA((2,)), pltpu.SemaphoreType.DMA,
        ],
        compiler_params=pltpu.CompilerParams(
            collective_id=6, has_side_effects=True, vmem_limit_bytes=VMEM_LIMIT
        ),
        name="first_norm_back",
    )(x, n1, dresb, dres, dq, a0, w0, perm, vec, vec2)


def allowed_pairs(shape, key_start, query_start):
    key = key_start + lax.broadcasted_iota(jnp.int32, shape, 0)
    query = query_start + lax.broadcasted_iota(jnp.int32, shape, 1)
    return key <= query


def transposed(values):
    return values.astype(F32).T


def spread(block, target, row, rows=64):
    target[pl.ds(row, 64), :] = block[:, 0:64]
    target[pl.ds(row + 64, 64), :] = block[:, 64:128]


def attend_kernel(info, r_ref, kv16, q16, dense_out, o_out, o16_out, l_out, l16_out, query, key, value, value_t, value16_t):
    rank, wraps = info[0], info[1]

    @pl.loop(0, 16)
    def _(b):
        row = pl.multiple_of(b * 128, 128)
        spread(r_ref[b, 0:64, :] * jnp.asarray(0.125, BF16), query, row)
        spread(r_ref[b, 64:128, :], key, row)
        spread(r_ref[b, 128:192, :], value, row)

    @pl.loop(0, 4)
    def _(b):
        rows = pl.ds(pl.multiple_of(b * KEYS, KEYS), KEYS)
        value_t[:, rows] = transposed(value[rows, :]).astype(BF16)
        value16_t[:, rows] = transposed(kv16[rows, :])[64:128].astype(BF16)

    def step(q, k_ref, v_t, j, carry, query_start=None):
        peak, running, mixed = carry
        rows = pl.ds(pl.multiple_of(j * KEYS, KEYS), KEYS)
        scores = dot_nt(k_ref[rows, 0:64], q)
        if query_start is not None:
            scores = jnp.where(allowed_pairs(scores.shape, j * KEYS, query_start), scores, masked_score)
        new_peak = jnp.maximum(peak, jnp.max(scores, axis=0, keepdims=True))
        shrink = jnp.exp(peak - new_peak)
        weights = jnp.exp(scores - new_peak)
        running = running * shrink + jnp.sum(weights, axis=0, keepdims=True)
        mixed = mixed * shrink + dot_nn(v_t[:, rows], weights.astype(BF16))
        return new_peak, running, mixed

    def empty(width):
        return (
            jnp.full((1, width), masked_score, F32), jnp.zeros((1, width), F32), jnp.zeros((64, width), F32)
        )

    @pl.loop(0, 4)
    def _(i):
        rows = pl.ds(pl.multiple_of(i * KEYS, KEYS), KEYS)
        q = query[rows, :]
        start = jnp.where((wraps == 1) & (i >= 2), 2, 0)
        carry = lax.fori_loop(
            start, i, lambda j, carry: step(q, key, value_t, j, carry), empty(KEYS)
        )
        peak, running, mixed = step(q, key, value_t, i, carry, i * KEYS)
        result = (mixed / running).T.astype(BF16)
        o_out[rows, :] = result
        for n in range(4):
            dense_out[2 * i + n // 2, :, 64 * (n % 2) : 64 * (n % 2) + 64] = result[128 * n : 128 * n + 128]
        l_out[:, rows] = peak + jnp.log(running)

    q = q16[...] * jnp.asarray(0.125, BF16)
    start = jnp.where((wraps == 1) & (rank >= 8), 2, 0)
    peak, running, mixed = lax.fori_loop(
        start, rank // 4 + 1,
        lambda j, carry: step(q, kv16, value16_t, j, carry, rank * QUARTER), empty(QUARTER),
    )
    o16_out[...] = (mixed / running).T.astype(BF16)
    l16_out[...] = peak + jnp.log(running)


def attend_call(info, r, kv16, q16):
    tokens = jax.ShapeDtypeStruct((SEQ, 64), BF16)
    return pl.pallas_call(
        attend_kernel,
        out_shape=(
            jax.ShapeDtypeStruct((8, 128, 128), BF16), tokens, jax.ShapeDtypeStruct((QUARTER, 64), BF16),
            jax.ShapeDtypeStruct((1, SEQ), F32), jax.ShapeDtypeStruct((1, QUARTER), F32), tokens, tokens, tokens,
        ),
        in_specs=[SMEM_SPEC, VMEM_SPEC, VMEM_SPEC, VMEM_SPEC],
        out_specs=(VMEM_SPEC,) * 8,
        scratch_shapes=[pltpu.VMEM((64, SEQ), BF16), pltpu.VMEM((64, SEQ), BF16)],
        compiler_params=pltpu.CompilerParams(vmem_limit_bytes=VMEM_LIMIT),
        name="attend_forward",
    )(info, r, kv16, q16)


def attend_back_kernel(
    info, query, key, value, kv16, q16, o_ref, o16, do_dense, do16, l_ref, l16,
    msg, part16, dq16_out, do_ref, key_t, key16_t, delta, dq_t,
):
    rank, wraps = info[0], info[1]

    @pl.loop(0, 16)
    def _(b):
        spread(do_dense[b], do_ref, pl.multiple_of(b * 128, 128))

    @pl.loop(0, 4)
    def _(b):
        rows = pl.ds(pl.multiple_of(b * KEYS, KEYS), KEYS)
        key_t[:, rows] = transposed(key[rows, :]).astype(BF16)
        key16_t[:, rows] = transposed(kv16[rows, :])[0:64].astype(BF16)
        product = do_ref[rows, :].astype(F32) * o_ref[rows, :].astype(F32)
        delta[:, rows] = jnp.sum(product.T, axis=0, keepdims=True)
        dq_t[:, rows] = jnp.zeros((64, KEYS), F32)

    def put(section, j, result):
        for n in range(4):
            for half in range(2):
                msg[4 * j + n, 64 * section : 64 * section + 64, 64 * half : 64 * half + 64] = result[
                    128 * n + 64 * half : 128 * n + 64 * half + 64
                ]

    def pair(keys, values, q, d_out, log_total, delta_row, mask):
        scores = dot_nt(keys, q)
        probs = jnp.exp(scores - log_total)
        if mask is not None:
            probs = jnp.where(mask(scores.shape), probs, 0.0)
        probs = probs.astype(BF16)
        d_prob = dot_nt(values, d_out)
        d_scores = (probs.astype(F32) * (d_prob - delta_row)).astype(BF16)
        return dot_nn(d_scores, q), dot_nn(probs, d_out), d_scores

    @pl.loop(0, 4)
    def _(j):
        rows = pl.ds(pl.multiple_of(j * KEYS, KEYS), KEYS)
        keys, values = key[rows, :], value[rows, :]

        def step(i, carry, mask=None):
            d_key, d_value = carry
            at = pl.ds(pl.multiple_of(i * KEYS, KEYS), KEYS)
            more_key, more_value, d_scores = pair(
                keys, values, query[at, :], do_ref[at, :], l_ref[:, at], delta[:, at], mask
            )
            dq_t[:, at] += dot_nn(key_t[:, rows], d_scores)
            return d_key + more_key, d_value + more_value

        zero = jnp.zeros((KEYS, 64), F32)
        carry = step(j, (zero, zero), lambda shape: allowed_pairs(shape, 0, 0))
        end = jnp.where((wraps == 1) & (j < 2), 2, 4)
        d_key, d_value = lax.fori_loop(j + 1, end, step, carry)
        put(1, j, d_key.astype(BF16))
        put(2, j, d_value.astype(BF16))

    q = q16[...] * jnp.asarray(0.125, BF16)
    d_out16 = do16[...]
    delta16 = jnp.sum((d_out16.astype(F32) * o16[...].astype(F32)).T, axis=0, keepdims=True)
    start = jnp.where((wraps == 1) & (rank >= 8), 2, 0)

    def last_step(j, dq):
        rows = pl.ds(pl.multiple_of(j * KEYS, KEYS), KEYS)
        d_key, d_value, d_scores = pair(
            kv16[rows, 0:64], kv16[rows, 64:128], q, d_out16, l16[...], delta16,
            lambda shape: allowed_pairs(shape, j * KEYS, rank * QUARTER),
        )
        part16[rows, 0:64] = d_key.astype(BF16)
        part16[rows, 64:128] = d_value.astype(BF16)
        return dq + dot_nn(key16_t[:, rows], d_scores)

    @pl.loop(0, 4)
    def _(j):
        rows = pl.ds(pl.multiple_of(j * KEYS, KEYS), KEYS)
        part16[rows, :] = jnp.zeros((KEYS, 128), BF16)
        put(0, j, (dq_t[:, rows] * 0.125).T.astype(BF16))

    dq = lax.fori_loop(start, rank // 4 + 1, last_step, jnp.zeros((64, QUARTER), F32))
    dq16_out[...] = (dq * 0.125).T.astype(BF16)


def attend_back_call(info, *args):
    return pl.pallas_call(
        attend_back_kernel,
        out_shape=(
            jax.ShapeDtypeStruct((16, 192, 128), BF16), jax.ShapeDtypeStruct((SEQ, 128), BF16),
            jax.ShapeDtypeStruct((QUARTER, 64), BF16),
        ),
        in_specs=[SMEM_SPEC] + [VMEM_SPEC] * 11,
        out_specs=(VMEM_SPEC,) * 3,
        scratch_shapes=[
            pltpu.VMEM((SEQ, 64), BF16), pltpu.VMEM((64, SEQ), BF16), pltpu.VMEM((64, SEQ), BF16),
            pltpu.VMEM((1, SEQ), F32), pltpu.VMEM((64, SEQ), F32),
        ],
        compiler_params=pltpu.CompilerParams(vmem_limit_bytes=VMEM_LIMIT),
        name="attend_backward",
    )(info, *args)


def packed_block(block):
    tail = jnp.pad(block[32:34], ((0, 0), (0, WIDE - D))).reshape(18, 128)
    return jnp.concatenate(
        [jnp.pad(block[:32], ((0, 0), (0, WIDE - D))), jnp.pad(tail, ((0, 14), (0, 0)))], axis=1
    )


def unpacked_block(packed):
    tail = packed[:18, WIDE:].reshape(2, WIDE)[:, :D]
    return jnp.concatenate([packed[:, :D], tail], axis=0)


def permutation():
    feature = jnp.arange(D, dtype=jnp.int32)
    block, inside = feature // 34, feature % 34
    place = jnp.where(inside < 32, 32 * block + inside, MAIN + 32 * (inside - 32) + block)
    chosen = place[:, None] == jnp.arange(WIDE, dtype=jnp.int32)[None, :]
    return chosen.astype(BF16).reshape(4, 272, WIDE)


def per_device(
    layer_input,
    first_norm_gain,
    first_norm_bias,
    w_qkv,
    w_out,
    second_norm_gain,
    second_norm_bias,
    w_up,
    w_down,
    gradient_of_output,
):
    row, col = lax.axis_index("row"), lax.axis_index("col")
    rank, core = (row + 2) % 4 * 4 + col, col % 2
    wraps = ((row < 2) | (row >= 30)).astype(jnp.int32)
    info = jnp.stack([rank, wraps]).astype(jnp.int32)
    perm = permutation()
    vectors = jnp.concatenate(
        [
            jnp.stack([first_norm_gain, first_norm_bias, second_norm_gain, second_norm_bias]),
            jnp.zeros((4, 272), F32),
        ]
    )
    blocks = (
        packed_block(jnp.concatenate([w_qkv, w_out.T], axis=1)),
        packed_block(w_up),
        packed_block(w_down.T),
    )
    w0, w1, w2, x4, g4, v4 = gather_all(blocks, layer_input.T, gradient_of_output.T, vectors)
    w0, w1, w2 = (w.reshape(2, MAIN, PACK) for w in (w0, w1, w2))
    x, n1, vec, message, last, q16 = qkv_call(x4, v4, perm, w0)
    heads, kv16 = qkv_exchange(message, last)
    kv16 = kv16.reshape(SEQ, 128)
    dense, o, o16, log_total, log16, query, key, value = attend_call(info, heads, kv16, q16)
    mixed, both16 = mixed_exchange(dense, o16)
    attn = jnp.concatenate(
        [
            mixed.reshape(16, QUARTER, 2, HEAD_DIM).transpose(2, 1, 0, 3).reshape(PAIR, 1024),
            both16.reshape(PAIR, HEAD_DIM),
        ],
        axis=1,
    ).reshape(PAIR, 2, 2, 272)
    attn = lax.dynamic_index_in_dim(attn, core, 2, keepdims=False)
    a0 = jnp.pad(attn.transpose(1, 0, 2), ((0, 0), (0, 0), (QKV_COLS, WIDE - D)))
    y4, dres, dresb, gr1, gr2, dmsg, do16, vec2 = middle_call(x, a0, w0, w1, w2, g4, perm, vec)
    do = grad_exchange(dmsg)
    back, part16, dq16 = attend_back_call(
        info, query, key, value, kv16, q16, o, o16, do, do16, log_total, log16
    )
    back, sums16 = back_exchange(back, part16.reshape(8, 2, QUARTER, 128))
    last_sums = jnp.sum(sums16.astype(F32), axis=0).astype(BF16)
    back = back.reshape(16, 3, 64, 2, HEAD_DIM).transpose(1, 3, 2, 0, 4).reshape(3, QUARTER, 1024)
    d_qkv = jnp.concatenate(
        [back[0], dq16, back[1], last_sums[:, :64], back[2], last_sums[:, 64:]], axis=1
    )
    dq0 = jnp.pad(
        d_qkv.reshape(QUARTER, 2, 2, QKV_COLS).transpose(2, 1, 0, 3), ((0, 0), (0, 0), (0, 0), (0, WIDE - QKV_COLS))
    )
    gin4, gr0, sums4 = first_call(x, n1, dresb, dres, dq0, a0, w0, perm, vec, vec2)
    grouped = tuple(g.reshape(2, 2, 4, 4, 32, PACK) for g in (gr0, gr1, gr2))
    sums, layer_output, gin, sums4 = scatter_all(grouped, y4, gin4, sums4)
    own_perm = lax.dynamic_index_in_dim(perm, col, 0, keepdims=False).astype(F32)
    vg = lax.dot_general(
        sums4, own_perm, (((1,), (1,)), ((), ())),
        preferred_element_type=F32, precision=lax.Precision.HIGHEST,
    )
    s0, s1, s2 = (unpacked_block(sums[n]) for n in range(3))
    return (
        layer_output.T,
        gin.T.astype(F32),
        vg[4],
        vg[5],
        s0[:, :QKV_COLS],
        s0[:, QKV_COLS:].T,
        vg[0],
        vg[1],
        s1,
        s2.T,
    )


def solution(mesh):
    placed = (
        P("row", "col"),
        P("col"),
        P("col"),
        P("row", "col"),
        P("col", "row"),
        P("col"),
        P("col"),
        P("row", "col"),
        P("col", "row"),
        P("row", "col"),
    )
    return jax.shard_map(
        per_device,
        mesh=mesh,
        in_specs=placed,
        out_specs=(
            P("row", "col"),
            P("row", "col"),
            P("col"),
            P("col"),
            P("row", "col"),
            P("col", "row"),
            P("col"),
            P("col"),
            P("row", "col"),
            P("col", "row"),
        ),
        check_vma=False,
    )
```

profile of v0, /device:TPU:1, one launch (start us, length us, event | category | flops | bytes accessed | tf_op | source)
XLA Modules:
  0.0 365.4 jit_solution(983261734210739418)
XLA Ops:
  4.0 0.8 fusion.23
  4.8 0.7 slice.122
  5.6 0.7 slice.93
  7.0 0.9 fusion.14
  7.9 0.9 slice.121
  9.4 0.9 slice.92
  11.0 2.4 iota_compare_fusion
  13.4 73.9 %gather_weights.1 = (bf16[2,2,4,4,32,1280]{5,4,3,2,1,0:T(8,128)(2,1)}, bf16[2,2,4,4,32,1280]{5,4,3,2,1,0:T(8,128)(2,1)}, bf16[2,2,4,4,32,1280]{5,4,3,2,1,0:T(8,1...) custom-call(bf16[32,1280]{1,0:T(8,128)(2,1)} %get-tuple-element.112.block0, ...), custom_call_target="tpu_custom_call" | custom-call | tf_op jit(solution)/shard_map/gather_weights/pallas_call | solution.py:232
  87.3 14.2 %norm_and_qkv.1 = (bf16[256,1152]{1,0:T(8,128)(2,1)}, bf16[256,1152]{1,0:T(8,128)(2,1)}, f32[8,1152]{1,0:T(8,128)}, bf16[16,192,128]{2,1,0:T(8,128)(2,1)}, bf16[...) custom-call(bf16[4,272,256]{2,1,0:T(8,128)(2,1)} %get-tuple-element.54.x4, f32[4,8,272]{2,1,0:T(8,128)} %get-tuple-element.55.v4, ...), custom_call_target="tpu_custom_call" | custom-call | tf_op jit(solution)/shard_map/norm_and_qkv/pallas_call | solution.py:844
  101.5 21.7 %exchange_qkv.1 = (bf16[16,192,128]{2,1,0:T(8,128)(2,1)}, bf16[16,128,128]{2,1,0:T(8,128)(2,1)}) custom-call(bf16[16,192,128]{2,1,0:T(8,128)(2,1)} %get-tuple-element.59.source, bf16[128,128]{1,0:T(8,128)(2,1)} %get-tuple-element.60.last), custom_call_target="tpu_custom_call" | custom-call | tf_op jit(solution)/shard_map/exchange_qkv/pallas_call | solution.py:323
  123.2 10.1 %attend_forward.1 = (bf16[8,128,128]{2,1,0:T(8,128)(2,1)}, bf16[2048,64]{1,0:T(8,128)(2,1)}, bf16[128,64]{1,0:T(8,128)(2,1)}, f32[1,2048]{1,0:T(1,128)}, f32[1,1...) custom-call(s32[2]{0:T(128)} %pad_add_fusion.info, ...), custom_call_target="tpu_custom_call" | custom-call | tf_op jit(solution)/shard_map/attend_forward/pallas_call | solution.py:1203
  133.3 15.4 %exchange_mixed.1 = (bf16[16,128,128]{2,1,0:T(8,128)(2,1)}, bf16[2,128,64]{2,1,0:T(8,128)(2,1)}) custom-call(bf16[8,128,128]{2,1,0:T(8,128)(2,1)} %get-tuple-element.64.source, bf16[128,64]{1,0:T(8,128)(2,1)} %get-tuple-element.65.last.o16), custom_call_target="tpu_custom_call" | custom-call | tf_op jit(solution)/shard_map/exchange_mixed/pallas_call | solution.py:323
  148.7 1.3 copy.20
  151.1 1.3 pad.47.a0
  152.4 48.5 %feed_forward.1 = (bf16[4,272,128]{2,1,0:T(8,128)(2,1)}, f32[256,1152]{1,0:T(8,128)}, bf16[256,1152]{1,0:T(8,128)(2,1)}, bf16[2,1024,1280]{2,1,0:T(8,128)(2,1)},...) custom-call(bf16[256,1152]{1,0:T(8,128)(2,1)} %get-tuple-element.57., ...), custom_call_target="tpu_custom_call" | custom-call | tf_op jit(solution)/shard_map/feed_forward/pallas_call | solution.py:1013
  201.0 12.3 %exchange_d_mix.1.do_dense = bf16[16,64,128]{2,1,0:T(8,128)(2,1)} custom-call(bf16[16,64,128]{2,1,0:T(8,128)(2,1)} %get-tuple-element.78.source), custom_call_target="tpu_custom_call" | custom-call | tf_op jit(solution)/shard_map/exchange_d_mix/pallas_call | solution.py:323
  213.3 12.3 %attend_backward.1 = (bf16[16,192,128]{2,1,0:T(8,128)(2,1)}, bf16[2048,128]{1,0:T(8,128)(2,1)}, bf16[128,64]{1,0:T(8,128)(2,1)}) custom-call(s32[2]{0:T(128)} %pad_add_fusion.info, bf16[2048,64]{1,0:T(8,128)(2,1)} %get-tuple-element.74.query, bf16[2048,64]{1,0:T(8,128)(2,1)} %get-tuple-element.75.key, bf16[2048,64]{1,0:T(8,128)(2,1)} %get-tuple-element.76.value, ...), custom_call_target="tpu_custom_call" | custom-call | tf_op jit(solution)/shard_map/attend_backward/pallas_call | solution.py:1300
  225.6 22.3 %exchange_d_qkv.1 = (bf16[16,192,128]{2,1,0:T(8,128)(2,1)}, bf16[8,128,128]{2,1,0:T(8,128)(2,1)}) custom-call(bf16[16,192,128]{2,1,0:T(8,128)(2,1)} %get-tuple-element.82.source, bf16[8,2,128,128]{3,2,1,0:T(8,128)(2,1)} %bitcast.78), custom_call_target="tpu_custom_call" | custom-call | tf_op jit(solution)/shard_map/exchange_d_qkv/pallas_call | solution.py:323
  247.9 1.0 reduce_sum.12
  249.0 3.2 reshape.143
  252.2 1.0 copy.30
  255.0 0.8 copy.25
  256.5 1.1 pad.48.dq_ref
  257.6 16.7 %first_norm_back.1 = (bf16[4,272,128]{2,1,0:T(8,128)(2,1)}, bf16[2,1024,1280]{2,1,0:T(8,128)(2,1)}, f32[8,1152]{1,0:T(8,128)}) custom-call(bf16[256,1152]{1,0:T(8,128)(2,1)} %get-tuple-element.57.x_ref, bf16[256,1152]{1,0:T(8,128)(2,1)} %get-tuple-element.58.n1, bf16[256,1152]{1,0:T(8,128)(2,1)} %get-tuple-element.72.dresb, ...), custom_call_target="tpu_custom_call" | custom-call | tf_op jit(solution)/shard_map/first_norm_back/pallas_call | solution.py:1105
  274.2 83.4 %scatter_gradients.1 = (f32[3,32,1280]{2,1,0:T(8,128)}, bf16[272,512]{1,0:T(8,128)(2,1)}, bf16[272,512]{1,0:T(8,128)(2,1)}, f32[8,1152]{1,0:T(8,128)}) custom-call(bf16[2,2,4,4,32,1280]{5,4,3,2,1,0:T(8,128)(2,1)} %bitcast.66, bf16[2,2,4,4,32,1280]{5,4,3,2,1,0:T(8,128)(2,1)} %bitcast.64, bf16[2,2,4,4,32,1280]{5,4,3,2,1,0:T(8,128)(2,1)} %bitcast.65, ...), custom_call_target="tpu_custom_call" | custom-call | tf_op jit(solution)/shard_map/scatter_gradients/pallas_call | solution.py:680
  357.6 1.4 fusion
  359.6 1.1 slice_bitcast_fusion
  360.9 0.7 pad_maximum_fusion.1
  361.6 0.7 maximum_bitcast_fusion
  362.3 0.7 fusion.15
  363.7 0.9 convert_bitcast_fusion
  364.5 0.7 copy.33
  (47 shorter events, 10.2 us)
Async XLA Ops:
  148.7 2.0 copy-start.2
  253.5 1.1 copy-start.3
  359.6 4.1 %copy-start.1 = (bf16[272,512]{1,0:T(8,128)(2,1)S(1)}, bf16[272,512]{1,0:T(8,128)(2,1)}, u32[]{:S(2)}) copy-start(bf16[272,512]{1,0:T(8,128)(2,1)} %get-tuple-element.95) | copy-start | bytes 835588
  360.8 3.8 %copy-start = (bf16[272,512]{1,0:T(8,128)(2,1)S(1)}, bf16[272,512]{1,0:T(8,128)(2,1)}, u32[]{:S(2)}) copy-start(bf16[272,512]{1,0:T(8,128)(2,1)} %get-tuple-element.94) | copy-start | bytes 835588
where the time goes:
time: 369 us; the launch traced here: 365 us
  Pallas kernels  331 us (90%)
  local copies, waits for them, and re-layouts  21.4 us (6%)
  other arithmetic  10.7 us (3%)
    pallas_call x1, Pallas kernels, scatter_all(): pl.pallas_call(scatter_kernel, out_shape=(jax.ShapeDtypeStruct((3, 32, PA...  83.4 us
    pallas_call x1, Pallas kernels, gather_all(): pl.pallas_call(gather_kernel, out_shape=(whole, whole, whole, tokens, tok...  73.9 us
    pallas_call x4, Pallas kernels, exchange_call(): pl.pallas_call(kernel, out_shape=outs, in_specs=in_specs or [ANY] * len(a...  71.7 us
    pallas_call x1, Pallas kernels, middle_call(): pl.pallas_call(middle_kernel, out_shape=(jax.ShapeDtypeStruct((4, 272, QU...  48.5 us
    pallas_call x1, Pallas kernels, first_call(): pl.pallas_call(first_kernel, out_shape=(jax.ShapeDtypeStruct((4, 272, QUA...  16.7 us
    pallas_call x1, Pallas kernels, qkv_call(): pl.pallas_call(qkv_kernel, out_shape=(row, row, jax.ShapeDtypeStruct((8,...  14.2 us
    pallas_call x1, Pallas kernels, attend_back_call(): pl.pallas_call(attend_back_kernel, out_shape=(jax.ShapeDtypeStruct((16, 1...  12.3 us
    pallas_call x1, Pallas kernels, attend_call(): pl.pallas_call(attend_kernel, out_shape=(jax.ShapeDtypeStruct((8, 128, 12...  10.1 us

commit v1 on v0

--- a/solution.py
+++ b/solution.py
@@ -366,71 +366,15 @@
     )
 
 
-def grad_exchange_kernel(source, target, send, recv, local):
-    group = Group()
-    group.greet()
-    group.finish(*group.all_to_all(source, target, send, recv, local))
-
-
-def grad_exchange(source):
-    outs = (jax.ShapeDtypeStruct((16, 64, 128), BF16),)
-    return exchange_call(grad_exchange_kernel, "exchange_d_mix", 7, outs, DIRECT, source)[0]
-
-
-def back_exchange_kernel(
-    source, parts, target, sums_out, send, recv, local, theirs, summed, swap_send, swap_recv, psend, precv, plocal
-):
-    group = Group()
-    group.greet()
-    swap = remote(parts.at[:, 1 - group.core], theirs, swap_send, swap_recv, group.partner)
-    swap.start()
-    direct = group.all_to_all(source, target, send, recv, local)
-    swap.wait_recv()
-
-    @pl.loop(0, 8)
-    def _(p):
-        summed[p] = (parts[p, group.core].astype(F32) + theirs[p].astype(F32)).astype(BF16)
-
-    own = pltpu.make_async_copy(summed.at[group.pair], sums_out.at[group.pair], plocal)
-    own.start()
-    sent = [swap]
-    for e in range(1, 8):
-        other = lax.rem(group.pair + e, 8)
-        copy = remote(
-            summed.at[other], sums_out.at[group.pair], psend.at[e], precv.at[e], group.device(other * 2 + group.core)
-        )
-        copy.start()
-        sent.append(copy)
-    for e in range(1, 8):
-        origin = lax.rem(group.pair + 8 - e, 8)
-        block = sums_out.at[origin]
-        remote(block, block, psend.at[e], precv.at[e], group.device(origin * 2 + group.core)).wait_recv()
-    group.finish(*direct)
-    for copy in sent:
-        copy.wait_send()
-    own.wait()
-
-
-def back_exchange(source, parts):
-    outs = (jax.ShapeDtypeStruct((16, 192, 128), BF16), jax.ShapeDtypeStruct((8, QUARTER, 128), BF16))
-    block = pltpu.VMEM((8, QUARTER, 128), BF16)
-    scratch = DIRECT + [block, block, pltpu.SemaphoreType.DMA, pltpu.SemaphoreType.DMA] + [
-        pltpu.SemaphoreType.DMA((8,)), pltpu.SemaphoreType.DMA((8,)), pltpu.SemaphoreType.DMA
-    ]
-    return exchange_call(
-        back_exchange_kernel, "exchange_d_qkv", 8, outs, scratch, source, parts, in_specs=[ANY, VMEM_SPEC]
-    )
-
-
 def free_axes(fixed):
     return [axis for axis in ("y", "z", "x") if axis not in fixed]
 
 
-def buffer_shape(fixed, rows):
+def buffer_shape(fixed, rows, width):
     shape = ()
     for axis in free_axes(fixed):
         shape = shape + ((2, 2) if axis == "y" else (4,))
-    return shape + (rows, PACK)
+    return shape + (rows, width)
 
 
 def buffer_index(at):
@@ -442,43 +386,199 @@
 
 
 VECTOR_AXES = ("z", "x", "y")
-
-
-def scatter_kernel(part0, part1, part2, y_ref, gin_ref, v_ref, out_ref, y_out, gin_out, v_out, *scratch):
+CHUNKS = (2, 1, 3, 0)
+
+
+class Reduction:
+    def __init__(self, me, source, widths, scratch, out):
+        self.me, self.source, self.widths, self.out = me, source, widths, out
+        self.offsets = (0, widths[0], widths[0] + widths[1])
+        self.sums = scratch[0:3]
+        self.halves, self.fulls = {}, {}
+        position = 3
+        for piece in range(3):
+            for stage in range(3):
+                self.halves[piece, stage] = scratch[position : position + 2]
+                self.fulls[piece, stage] = scratch[position + 2 : position + 4]
+                position += 4
+        self.local, self.big_send, self.big_recv, self.send, self.recv = scratch[position : position + 5]
+        self.sent, self.loads = [], {}
+
+    @staticmethod
+    def scratch(widths):
+        found = [pltpu.VMEM((2, 2, 4, 4, 32, width), BF16) for width in widths]
+        for piece in range(3):
+            order = SCATTER_ORDERS[piece]
+            for stage in range(3):
+                fixed = order[: stage + 1]
+                found += [pltpu.VMEM(buffer_shape(fixed, 16, widths[piece]), BF16) for _ in range(2)]
+                found += [pltpu.VMEM(buffer_shape(fixed, 32, widths[piece]), BF16) for _ in range(2)]
+        found += [pltpu.SemaphoreType.DMA((3, 4, 4))] * 3 + [pltpu.SemaphoreType.DMA((3, 2, 4))] * 2
+        return found
+
+    def shifted(self, axis, distance):
+        return lax.rem(self.me.at[axis] + distance, 4)
+
+    def load_all(self):
+        for k in range(4):
+            for u in range(4):
+                for piece in range(3):
+                    first, second = SCATTER_ORDERS[piece][:2]
+                    index = place_index(
+                        {first: self.shifted(first, CHUNKS[k]), second: self.shifted(second, CHUNKS[u])}
+                    )
+                    lanes = pl.ds(self.offsets[piece], self.widths[piece])
+                    load = pltpu.make_async_copy(
+                        self.source.at[index + (everything(), lanes)], self.sums[piece].at[index],
+                        self.local.at[piece, k, u],
+                    )
+                    load.start()
+                    self.loads[piece, k, u] = load
+
+    def stage_fixed(self, piece, stage):
+        return {axis: self.me.at[axis] for axis in SCATTER_ORDERS[piece][:stage]}
+
+    def each_tile(self, fixed, body):
+        axes = free_axes(fixed)
+        count = 4 ** len(axes)
+        if count == 1:
+            body({})
+            return
+
+        @pl.loop(0, count)
+        def _(t):
+            body({axes[0]: t})
+
+    def chunk(self, piece, stage, u):
+        if stage > 0:
+            return {}
+        axis = SCATTER_ORDERS[piece][1]
+        return {axis: self.shifted(axis, CHUNKS[u])}
+
+    def sems(self, piece, stage, n, u):
+        if stage == 0:
+            return self.big_send.at[piece, u, n], self.big_recv.at[piece, u, n]
+        return self.send.at[piece, stage - 1, n], self.recv.at[piece, stage - 1, n]
+
+    def part_of(self, buffer, piece, stage, u):
+        if stage > 0:
+            return buffer
+        axis = SCATTER_ORDERS[piece][1]
+        value = self.shifted(axis, CHUNKS[u])
+        index = ()
+        for name in free_axes({SCATTER_ORDERS[piece][0]: 0}):
+            if name == "y":
+                index += (lax.rem(value, 2), value // 2) if name == axis else (everything(), everything())
+            else:
+                index += (value,) if name == axis else (everything(),)
+        return buffer.at[index]
+
+    def start(self, source, target, semaphores, axis, n):
+        copy = remote(source, target, *semaphores, self.me.step(axis, (1, -1)[n]))
+        copy.start()
+        self.sent.append(copy)
+
+    def wait(self, there, semaphores, axis):
+        remote(there, there, *semaphores, self.me.step(axis, 1)).wait_recv()
+
+    def begin(self, piece, stage, u=0):
+        if stage == 0:
+            self.loads[piece, 0, u].wait()
+        axis = SCATTER_ORDERS[piece][stage]
+        fixed = {**self.stage_fixed(piece, stage), axis: self.shifted(axis, 2), **self.chunk(piece, stage, u)}
+        for n in range(2):
+            self.start(
+                self.sums[piece].at[place_index(fixed) + (pl.ds(16 * n, 16),)],
+                self.part_of(self.halves[piece, stage][n], piece, stage, u), self.sems(piece, stage, n, u), axis, n,
+            )
+
+    def middle(self, piece, stage, n, u=0):
+        if stage == 0:
+            self.loads[piece, 1 + n, u].wait()
+        axis = SCATTER_ORDERS[piece][stage]
+        more = self.chunk(piece, stage, u)
+        fixed = {**self.stage_fixed(piece, stage), axis: self.shifted(axis, (1, 3)[n]), **more}
+        half, sums = self.halves[piece, stage][n], self.sums[piece]
+        self.wait(self.part_of(half, piece, stage, u), self.sems(piece, stage, n, u), axis)
+
+        def body(at):
+            index = place_index({**fixed, **at}) + (pl.ds(16 * n, 16),)
+            total = sums[index].astype(F32) + half[buffer_index({**more, **at})].astype(F32)
+            sums[index] = total.astype(BF16)
+
+        self.each_tile(fixed, body)
+        self.start(
+            sums.at[place_index(fixed)], self.part_of(self.fulls[piece, stage][n], piece, stage, u),
+            self.sems(piece, stage, 2 + n, u), axis, n,
+        )
+
+    def finish(self, piece, stage, u=0):
+        if stage == 0:
+            self.loads[piece, 3, u].wait()
+        axis = SCATTER_ORDERS[piece][stage]
+        more = self.chunk(piece, stage, u)
+        fixed = {**self.stage_fixed(piece, stage), axis: self.me.at[axis], **more}
+        first, second = self.fulls[piece, stage]
+        sums = self.sums[piece]
+        for n, buffer in enumerate((first, second)):
+            self.wait(self.part_of(buffer, piece, stage, u), self.sems(piece, stage, 2 + n, u), axis)
+
+        def body(at):
+            index = place_index({**fixed, **at})
+            if stage == 2:
+                total = sums[index].astype(F32) + (first[...].astype(F32) + second[...].astype(F32))
+                self.out[:, self.offsets[piece] : self.offsets[piece] + self.widths[piece]] = total
+            else:
+                place = buffer_index({**more, **at})
+                total = sums[index].astype(F32) + (first[place].astype(F32) + second[place].astype(F32))
+                sums[index] = total.astype(BF16)
+
+        self.each_tile(fixed, body)
+
+    def begin_chunk(self, u):
+        for piece in range(3):
+            self.begin(piece, 0, u)
+
+    def middle_chunk(self, u):
+        for n in range(2):
+            for piece in range(3):
+                self.middle(piece, 0, n, u)
+
+    def finish_chunk(self, u):
+        for piece in range(3):
+            self.finish(piece, 0, u)
+            if u == 0:
+                self.begin(piece, 1)
+            elif u < 3:
+                self.middle(piece, 1, u - 1)
+            else:
+                self.finish(piece, 1)
+                self.begin(piece, 2)
+
+    def finish_all(self):
+        for n in range(2):
+            for piece in range(3):
+                self.middle(piece, 2, n)
+        for piece in range(3):
+            self.finish(piece, 2)
+
+    def wait_sent(self):
+        for copy in self.sent:
+            copy.wait_send()
+
+
+LATE_WIDTHS = (512, 384, 384)
+EARLY_WIDTHS = (896, 896, 768)
+
+
+def scatter_kernel(source, y_ref, gin_ref, v_ref, out_ref, y_out, gin_out, v_out, *scratch):
     me = Place()
-    parts = (part0, part1, part2)
-    sums = scratch[0:3]
-    halves = {}
-    fulls = {}
-    position = 3
-    for piece in range(3):
-        for stage in range(3):
-            halves[piece, stage] = scratch[position : position + 2]
-            fulls[piece, stage] = scratch[position + 2 : position + 4]
-            position += 4
-    vectors = scratch[position : position + 3]
-    position += 3
-    local, big_send, big_recv, send, recv, out_send, out_recv, out_local, v_send, v_recv = scratch[position:]
+    vectors = scratch[0:3]
+    out_send, out_recv, out_local, v_send, v_recv = scratch[3:8]
+    reduction = Reduction(me, source, LATE_WIDTHS, scratch[8:], out_ref)
     greet(me.neighbours() + [me.step(axis, 2) for axis in VECTOR_AXES])
-
-    sent, loads = [], {}
-    for k in range(3):
-        for u in range(4):
-            for piece in range(3):
-                first, second = SCATTER_ORDERS[piece][:2]
-                index = place_index(
-                    {first: lax.rem(me.at[first] + (2, 1, 3)[k], 4), second: lax.rem(me.at[second] + (2, 1, 3, 0)[u], 4)}
-                )
-                load = pltpu.make_async_copy(parts[piece].at[index], sums[piece].at[index], local.at[piece, k, u])
-                load.start()
-                loads[piece, k, u] = load
-    for u in range(4):
-        for piece in range(3):
-            first, second = SCATTER_ORDERS[piece][:2]
-            index = place_index({first: me.at[first], second: lax.rem(me.at[second] + (2, 1, 3, 0)[u], 4)})
-            load = pltpu.make_async_copy(parts[piece].at[index], sums[piece].at[index], local.at[piece, 3, u])
-            load.start()
-            loads[piece, 3, u] = load
+    sent = []
+    reduction.load_all()
 
     def vectors_begin(phase, value):
         axis = VECTOR_AXES[phase]
@@ -501,107 +601,9 @@
         buffer = vectors[phase]
         return (buffer[0] + buffer[1]) + (buffer[2] + buffer[3])
 
-    def stage_fixed(piece, stage):
-        return {axis: me.at[axis] for axis in SCATTER_ORDERS[piece][:stage]}
-
-    def each_tile(fixed, body):
-        axes = free_axes(fixed)
-        count = 4 ** len(axes)
-        if count == 1:
-            body({})
-            return
-
-        @pl.loop(0, count)
-        def _(t):
-            if len(axes) == 1:
-                body({axes[0]: t})
-            else:
-                body({axes[0]: t // 4, axes[1]: lax.rem(t, 4)})
-
-    def chunk(piece, stage, u):
-        if stage > 0:
-            return {}
-        axis = SCATTER_ORDERS[piece][1]
-        return {axis: lax.rem(me.at[axis] + (2, 1, 3, 0)[u], 4)}
-
-    def sems(piece, stage, n, u):
-        if stage == 0:
-            return big_send.at[piece, u, n], big_recv.at[piece, u, n]
-        return send.at[piece, stage - 1, n], recv.at[piece, stage - 1, n]
-
-    def part_of(buffer, piece, stage, u):
-        if stage > 0:
-            return buffer
-        axis = SCATTER_ORDERS[piece][1]
-        value = lax.rem(me.at[axis] + (2, 1, 3, 0)[u], 4)
-        index = ()
-        for name in free_axes({SCATTER_ORDERS[piece][0]: 0}):
-            if name == "y":
-                index += (lax.rem(value, 2), value // 2) if name == axis else (everything(), everything())
-            else:
-                index += (value,) if name == axis else (everything(),)
-        return buffer.at[index]
-
-    def begin(piece, stage, u=0):
-        axis = SCATTER_ORDERS[piece][stage]
-        fixed = {**stage_fixed(piece, stage), axis: lax.rem(me.at[axis] + 2, 4), **chunk(piece, stage, u)}
-        for n in range(2):
-            copy = remote(
-                sums[piece].at[place_index(fixed) + (pl.ds(16 * n, 16),)],
-                part_of(halves[piece, stage][n], piece, stage, u),
-                *sems(piece, stage, n, u), me.step(axis, (1, -1)[n]),
-            )
-            copy.start()
-            sent.append(copy)
-
-    def middle(piece, stage, n, u=0):
-        axis = SCATTER_ORDERS[piece][stage]
-        more = chunk(piece, stage, u)
-        fixed = {**stage_fixed(piece, stage), axis: lax.rem(me.at[axis] + (1, 3)[n], 4), **more}
-        half = halves[piece, stage][n]
-        there = part_of(half, piece, stage, u)
-        remote(there, there, *sems(piece, stage, n, u), me.step(axis, 1)).wait_recv()
-
-        def body(at):
-            index = place_index({**fixed, **at}) + (pl.ds(16 * n, 16),)
-            total = sums[piece][index].astype(F32) + half[buffer_index({**more, **at})].astype(F32)
-            sums[piece][index] = total.astype(BF16)
-
-        each_tile(fixed, body)
-        copy = remote(
-            sums[piece].at[place_index(fixed)], part_of(fulls[piece, stage][n], piece, stage, u),
-            *sems(piece, stage, 2 + n, u), me.step(axis, (1, -1)[n]),
-        )
-        copy.start()
-        sent.append(copy)
-
-    def finish(piece, stage, u=0):
-        axis = SCATTER_ORDERS[piece][stage]
-        more = chunk(piece, stage, u)
-        fixed = {**stage_fixed(piece, stage), axis: me.at[axis], **more}
-        first, second = fulls[piece, stage]
-        for n, buffer in enumerate((first, second)):
-            there = part_of(buffer, piece, stage, u)
-            remote(there, there, *sems(piece, stage, 2 + n, u), me.step(axis, 1)).wait_recv()
-
-        def body(at):
-            index = place_index({**fixed, **at})
-            place = buffer_index({**more, **at})
-            if stage == 2:
-                total = sums[piece][index].astype(F32) + (first[...].astype(F32) + second[...].astype(F32))
-                out_ref[piece] = total
-            else:
-                total = sums[piece][index].astype(F32) + (first[place].astype(F32) + second[place].astype(F32))
-                sums[piece][index] = total.astype(BF16)
-
-        each_tile(fixed, body)
-
-    for u in range(4):
-        for piece in range(3):
-            loads[piece, 0, u].wait()
-            begin(piece, 0, u)
+    reduction.begin_chunk(0)
     vectors_begin(0, v_ref[...])
-
+    reduction.begin_chunk(1)
     pairs = ((y_ref, y_out), (gin_ref, gin_out))
     arrivals, own_copies = [], []
     for n, (source, target) in enumerate(pairs):
@@ -617,59 +619,29 @@
             sent.append(copy)
             origin = pl.ds(pl.multiple_of(lax.rem(me.col + 4 - distance, 4) * QUARTER, QUARTER), QUARTER)
             arrivals.append(remote(source.at[me.col], target.at[:, origin], *semaphore, peer))
-
-    def finish_chunk(u):
-        for piece in range(3):
-            loads[piece, 3, u].wait()
-            finish(piece, 0, u)
-            if u == 0:
-                begin(piece, 1)
-            elif u < 3:
-                middle(piece, 1, u - 1)
-            else:
-                finish(piece, 1)
-                begin(piece, 2)
-
     for u in range(4):
-        for n in range(2):
-            for piece in range(3):
-                loads[piece, 1 + n, u].wait()
-                middle(piece, 0, n, u)
+        reduction.middle_chunk(u)
         if u < 2:
+            reduction.begin_chunk(u + 2)
             vectors_begin(u + 1, vectors_end(u))
         if u == 3:
             v_out[...] = vectors_end(2)
         if u > 0:
-            finish_chunk(u - 1)
-    finish_chunk(3)
-    for n in range(2):
-        for piece in range(3):
-            middle(piece, 2, n)
-    for piece in range(3):
-        finish(piece, 2)
+            reduction.finish_chunk(u - 1)
+    reduction.finish_chunk(3)
+    reduction.finish_all()
     for copy in arrivals:
         copy.wait_recv()
     for copy in own_copies:
         copy.wait()
     for copy in sent:
         copy.wait_send()
-
-
-def scatter_all(parts, y4, gin4, vectors):
-    scratch = [pltpu.VMEM((2, 2, 4, 4, 32, PACK), BF16) for _ in range(3)]
-    for piece in range(3):
-        order = SCATTER_ORDERS[piece]
-        for stage in range(3):
-            fixed = order[: stage + 1]
-            scratch += [pltpu.VMEM(buffer_shape(fixed, 16), BF16) for _ in range(2)]
-            scratch += [pltpu.VMEM(buffer_shape(fixed, 32), BF16) for _ in range(2)]
-    scratch += [pltpu.VMEM((4, 8, WIDE), F32) for _ in range(3)]
+    reduction.wait_sent()
+
+
+def scatter_all(part, y4, gin4, vectors):
+    scratch = [pltpu.VMEM((4, 8, WIDE), F32) for _ in range(3)]
     scratch += [
-        pltpu.SemaphoreType.DMA((3, 4, 4)),
-        pltpu.SemaphoreType.DMA((3, 4, 4)),
-        pltpu.SemaphoreType.DMA((3, 4, 4)),
-        pltpu.SemaphoreType.DMA((3, 2, 4)),
-        pltpu.SemaphoreType.DMA((3, 2, 4)),
         pltpu.SemaphoreType.DMA((2, 3)),
         pltpu.SemaphoreType.DMA((2, 3)),
         pltpu.SemaphoreType.DMA((2,)),
@@ -679,15 +651,15 @@
     back = jax.ShapeDtypeStruct((272, 512), BF16)
     return pl.pallas_call(
         scatter_kernel,
-        out_shape=(jax.ShapeDtypeStruct((3, 32, PACK), F32), back, back, jax.ShapeDtypeStruct((8, WIDE), F32)),
-        in_specs=[ANY] * 5 + [VMEM_SPEC],
+        out_shape=(jax.ShapeDtypeStruct((32, PACK), F32), back, back, jax.ShapeDtypeStruct((8, WIDE), F32)),
+        in_specs=[ANY] * 3 + [VMEM_SPEC],
         out_specs=(VMEM_SPEC, ANY, ANY, VMEM_SPEC),
-        scratch_shapes=scratch,
+        scratch_shapes=scratch + Reduction.scratch(LATE_WIDTHS),
         compiler_params=pltpu.CompilerParams(
             collective_id=3, has_side_effects=True, vmem_limit_bytes=VMEM_LIMIT
         ),
         name="scatter_gradients",
-    )(*parts, y4, gin4, vectors)
+    )(part, y4, gin4, vectors)
 
 
 def unpack_tail(packed, tiles, wide, tail):
@@ -896,7 +868,7 @@
 
 def middle_kernel(
     x_ref, a0, w0_ref, w1_ref, w2_ref, g4, perm, vec,
-    y4, dres_out, dresb_out, gr1_out, gr2_out, dmsg, dlast, vec_out,
+    y4, dres_out, dresb_out, gr12_out, dmsg, dlast, vec_out,
     w0, w1, w2, gr1, gr2, resid, normed2, inverse2, n2, n2_t, cot, cot_t, total_t, dn2_t, hidden, dpre, turn1, turn2,
     dmix, tiles, out_tiles, tail1, tail2, tail_sum, mine1, theirs1, mine2, theirs2, mine_y, theirs_y, dmix_out,
     load, store, send, recv, local,
@@ -955,8 +927,8 @@
             third.start()
         weight_gradient(n2_t, dpre, out_tiles, tail_sum, gr1.at[j])
         weight_gradient(cot_t, hidden, out_tiles, tail_sum, gr2.at[j])
-        for n, (source, target) in enumerate(((gr1, gr1_out), (gr2, gr2_out))):
-            copy = pltpu.make_async_copy(source.at[j], target.at[j], store.at[n, j])
+        for n, source in enumerate((gr1, gr2)):
+            copy = pltpu.make_async_copy(source.at[j], gr12_out.at[j, :, pl.ds(PACK * n, PACK)], store.at[n, j])
             copy.start()
             stores.append(copy)
     grad = swap_end(second, mine2, theirs2).T
@@ -1004,7 +976,6 @@
 
 
 def middle_call(x, a0, w0, w1, w2, g4, perm, vec):
-    packed = jax.ShapeDtypeStruct((2, MAIN, PACK), BF16)
     weights = pltpu.VMEM((2, MAIN, PACK), BF16)
     row_f, row_b = pltpu.VMEM((PAIR, WIDE), F32), pltpu.VMEM((PAIR, WIDE), BF16)
     turn_f, turn_b = pltpu.VMEM((WIDE, PAIR), F32), pltpu.VMEM((WIDE, PAIR), BF16)
@@ -1014,12 +985,12 @@
         middle_kernel,
         out_shape=(
             jax.ShapeDtypeStruct((4, 272, QUARTER), BF16), jax.ShapeDtypeStruct((PAIR, WIDE), F32),
-            jax.ShapeDtypeStruct((PAIR, WIDE), BF16), packed, packed,
+            jax.ShapeDtypeStruct((PAIR, WIDE), BF16), jax.ShapeDtypeStruct((2, MAIN, 2 * PACK), BF16),
             jax.ShapeDtypeStruct((16, 64, 128), BF16), jax.ShapeDtypeStruct((QUARTER, 64), BF16),
             jax.ShapeDtypeStruct((8, WIDE), F32),
         ),
         in_specs=[VMEM_SPEC, VMEM_SPEC, ANY, ANY, ANY, VMEM_SPEC, VMEM_SPEC, VMEM_SPEC],
-        out_specs=(VMEM_SPEC, VMEM_SPEC, VMEM_SPEC, ANY, ANY, VMEM_SPEC, VMEM_SPEC, VMEM_SPEC),
+        out_specs=(VMEM_SPEC, VMEM_SPEC, VMEM_SPEC, ANY, VMEM_SPEC, VMEM_SPEC, VMEM_SPEC),
         scratch_shapes=[
             weights, weights, weights, weights, weights, row_f, row_f, pltpu.VMEM((PAIR, 128), F32), row_b, turn_b,
             row_b, turn_b, turn_f, turn_f, row_b, row_b, turn_b, turn_b, pltpu.VMEM((2, PAIR, 384), BF16),
@@ -1215,23 +1186,40 @@
 
 
 def attend_back_kernel(
-    info, query, key, value, kv16, q16, o_ref, o16, do_dense, do16, l_ref, l16,
-    msg, part16, dq16_out, do_ref, key_t, key16_t, delta, dq_t,
+    dmsg, gradients, query, key, value, kv16, q16, o_ref, o16, do16, l_ref, l16,
+    back_out, sums_out, dq16_out, reduced,
+    do_dense, msg, part16, theirs, summed, do_ref, key_t, key16_t, delta, dq_t,
+    send1, recv1, local1, send2, recv2, local2, swap_send, swap_recv, psend, precv, plocal, *scratch,
 ):
-    rank, wraps = info[0], info[1]
-
-    @pl.loop(0, 16)
-    def _(b):
-        spread(do_dense[b], do_ref, pl.multiple_of(b * 128, 128))
+    me, group = Place(), Group()
+    rank = group.rank
+    wraps = (group.row < 2) | (group.row >= 30)
+    reduction = Reduction(me, gradients, EARLY_WIDTHS, scratch, reduced)
+    greet([group.device(lax.rem(rank + d, 16)) for d in range(1, 16)] + me.neighbours())
+    first = group.all_to_all(dmsg, do_dense, send1, recv1, local1)
+    reduction.load_all()
+    reduction.begin_chunk(0)
 
     @pl.loop(0, 4)
     def _(b):
         rows = pl.ds(pl.multiple_of(b * KEYS, KEYS), KEYS)
         key_t[:, rows] = transposed(key[rows, :]).astype(BF16)
         key16_t[:, rows] = transposed(kv16[rows, :])[0:64].astype(BF16)
+        dq_t[:, rows] = jnp.zeros((64, KEYS), F32)
+
+    group.finish(*first)
+    for u in (1, 2, 3):
+        reduction.begin_chunk(u)
+
+    @pl.loop(0, 16)
+    def _(b):
+        spread(do_dense[b], do_ref, pl.multiple_of(b * 128, 128))
+
+    @pl.loop(0, 4)
+    def _(b):
+        rows = pl.ds(pl.multiple_of(b * KEYS, KEYS), KEYS)
         product = do_ref[rows, :].astype(F32) * o_ref[rows, :].astype(F32)
         delta[:, rows] = jnp.sum(product.T, axis=0, keepdims=True)
-        dq_t[:, rows] = jnp.zeros((64, KEYS), F32)
 
     def put(section, j, result):
         for n in range(4):
@@ -1250,8 +1238,7 @@
         d_scores = (probs.astype(F32) * (d_prob - delta_row)).astype(BF16)
         return dot_nn(d_scores, q), dot_nn(probs, d_out), d_scores
 
-    @pl.loop(0, 4)
-    def _(j):
+    def key_block(j):
         rows = pl.ds(pl.multiple_of(j * KEYS, KEYS), KEYS)
         keys, values = key[rows, :], value[rows, :]
 
@@ -1266,7 +1253,7 @@
 
         zero = jnp.zeros((KEYS, 64), F32)
         carry = step(j, (zero, zero), lambda shape: allowed_pairs(shape, 0, 0))
-        end = jnp.where((wraps == 1) & (j < 2), 2, 4)
+        end = jnp.where(wraps & (j < 2), 2, 4)
         d_key, d_value = lax.fori_loop(j + 1, end, step, carry)
         put(1, j, d_key.astype(BF16))
         put(2, j, d_value.astype(BF16))
@@ -1274,7 +1261,7 @@
     q = q16[...] * jnp.asarray(0.125, BF16)
     d_out16 = do16[...]
     delta16 = jnp.sum((d_out16.astype(F32) * o16[...].astype(F32)).T, axis=0, keepdims=True)
-    start = jnp.where((wraps == 1) & (rank >= 8), 2, 0)
+    start = jnp.where(wraps & (rank >= 8), 2, 0)
 
     def last_step(j, dq):
         rows = pl.ds(pl.multiple_of(j * KEYS, KEYS), KEYS)
@@ -1282,36 +1269,89 @@
             kv16[rows, 0:64], kv16[rows, 64:128], q, d_out16, l16[...], delta16,
             lambda shape: allowed_pairs(shape, j * KEYS, rank * QUARTER),
         )
-        part16[rows, 0:64] = d_key.astype(BF16)
-        part16[rows, 64:128] = d_value.astype(BF16)
+        for n in range(4):
+            block = part16.at[2 * j + n // 2, n % 2]
+            block[:, 0:64] = d_key[128 * n : 128 * n + 128].astype(BF16)
+            block[:, 64:128] = d_value[128 * n : 128 * n + 128].astype(BF16)
         return dq + dot_nn(key16_t[:, rows], d_scores)
+
+    part16[...] = jnp.zeros_like(part16)
+    dq = lax.fori_loop(start, rank // 4 + 1, last_step, jnp.zeros((64, QUARTER), F32))
+    dq16_out[...] = (dq * 0.125).T.astype(BF16)
+    swap = remote(part16.at[:, 1 - group.core], theirs, swap_send, swap_recv, group.partner)
+    swap.start()
+
+    @pl.loop(0, 2)
+    def _(j):
+        key_block(j)
+
+    reduction.middle_chunk(0)
+
+    @pl.loop(2, 4)
+    def _(j):
+        key_block(j)
 
     @pl.loop(0, 4)
     def _(j):
         rows = pl.ds(pl.multiple_of(j * KEYS, KEYS), KEYS)
-        part16[rows, :] = jnp.zeros((KEYS, 128), BF16)
         put(0, j, (dq_t[:, rows] * 0.125).T.astype(BF16))
 
-    dq = lax.fori_loop(start, rank // 4 + 1, last_step, jnp.zeros((64, QUARTER), F32))
-    dq16_out[...] = (dq * 0.125).T.astype(BF16)
-
-
-def attend_back_call(info, *args):
+    second = group.all_to_all(msg, back_out, send2, recv2, local2)
+    swap.wait_recv()
+
+    @pl.loop(0, 8)
+    def _(p):
+        summed[p] = (part16[p, group.core].astype(F32) + theirs[p].astype(F32)).astype(BF16)
+
+    own = pltpu.make_async_copy(summed.at[group.pair], sums_out.at[group.pair], plocal)
+    own.start()
+    sent = [swap]
+    for e in range(1, 8):
+        other = lax.rem(group.pair + e, 8)
+        copy = remote(
+            summed.at[other], sums_out.at[group.pair], psend.at[e], precv.at[e], group.device(other * 2 + group.core)
+        )
+        copy.start()
+        sent.append(copy)
+    for u in range(1, 4):
+        reduction.middle_chunk(u)
+        reduction.finish_chunk(u - 1)
+    reduction.finish_chunk(3)
+    reduction.finish_all()
+    for e in range(1, 8):
+        origin = lax.rem(group.pair + 8 - e, 8)
+        block = sums_out.at[origin]
+        remote(block, block, psend.at[e], precv.at[e], group.device(origin * 2 + group.core)).wait_recv()
+    group.finish(*second)
+    for copy in sent:
+        copy.wait_send()
+    own.wait()
+    reduction.wait_sent()
+
+
+def attend_back_call(*args):
+    block = pltpu.VMEM((8, QUARTER, 128), BF16)
+    eight = pltpu.SemaphoreType.DMA((8,))
+    one = pltpu.SemaphoreType.DMA
     return pl.pallas_call(
         attend_back_kernel,
         out_shape=(
-            jax.ShapeDtypeStruct((16, 192, 128), BF16), jax.ShapeDtypeStruct((SEQ, 128), BF16),
-            jax.ShapeDtypeStruct((QUARTER, 64), BF16),
+            jax.ShapeDtypeStruct((16, 192, 128), BF16), jax.ShapeDtypeStruct((8, QUARTER, 128), BF16),
+            jax.ShapeDtypeStruct((QUARTER, 64), BF16), jax.ShapeDtypeStruct((32, 2 * PACK), F32),
         ),
-        in_specs=[SMEM_SPEC] + [VMEM_SPEC] * 11,
-        out_specs=(VMEM_SPEC,) * 3,
+        in_specs=[ANY, ANY] + [VMEM_SPEC] * 10,
+        out_specs=(ANY, ANY, VMEM_SPEC, VMEM_SPEC),
         scratch_shapes=[
+            pltpu.VMEM((16, 64, 128), BF16), pltpu.VMEM((16, 192, 128), BF16), pltpu.VMEM((8, 2, QUARTER, 128), BF16),
+            block, block,
             pltpu.VMEM((SEQ, 64), BF16), pltpu.VMEM((64, SEQ), BF16), pltpu.VMEM((64, SEQ), BF16),
             pltpu.VMEM((1, SEQ), F32), pltpu.VMEM((64, SEQ), F32),
-        ],
-        compiler_params=pltpu.CompilerParams(vmem_limit_bytes=VMEM_LIMIT),
+        ] + DIRECT + DIRECT + [one, one, eight, eight, one] + Reduction.scratch(EARLY_WIDTHS),
+        compiler_params=pltpu.CompilerParams(
+            collective_id=7, has_side_effects=True, vmem_limit_bytes=VMEM_LIMIT
+        ),
         name="attend_backward",
-    )(info, *args)
+    )(*args)
 
 
 def packed_block(block):
@@ -1378,12 +1418,10 @@
     ).reshape(PAIR, 2, 2, 272)
     attn = lax.dynamic_index_in_dim(attn, core, 2, keepdims=False)
     a0 = jnp.pad(attn.transpose(1, 0, 2), ((0, 0), (0, 0), (QKV_COLS, WIDE - D)))
-    y4, dres, dresb, gr1, gr2, dmsg, do16, vec2 = middle_call(x, a0, w0, w1, w2, g4, perm, vec)
-    do = grad_exchange(dmsg)
-    back, part16, dq16 = attend_back_call(
-        info, query, key, value, kv16, q16, o, o16, do, do16, log_total, log16
+    y4, dres, dresb, gr12, dmsg, do16, vec2 = middle_call(x, a0, w0, w1, w2, g4, perm, vec)
+    back, sums16, dq16, early = attend_back_call(
+        dmsg, gr12.reshape(2, 2, 4, 4, 32, 2 * PACK), query, key, value, kv16, q16, o, o16, do16, log_total, log16
     )
-    back, sums16 = back_exchange(back, part16.reshape(8, 2, QUARTER, 128))
     last_sums = jnp.sum(sums16.astype(F32), axis=0).astype(BF16)
     back = back.reshape(16, 3, 64, 2, HEAD_DIM).transpose(1, 3, 2, 0, 4).reshape(3, QUARTER, 1024)
     d_qkv = jnp.concatenate(
@@ -1393,14 +1431,13 @@
         d_qkv.reshape(QUARTER, 2, 2, QKV_COLS).transpose(2, 1, 0, 3), ((0, 0), (0, 0), (0, 0), (0, WIDE - QKV_COLS))
     )
     gin4, gr0, sums4 = first_call(x, n1, dresb, dres, dq0, a0, w0, perm, vec, vec2)
-    grouped = tuple(g.reshape(2, 2, 4, 4, 32, PACK) for g in (gr0, gr1, gr2))
-    sums, layer_output, gin, sums4 = scatter_all(grouped, y4, gin4, sums4)
+    late, layer_output, gin, sums4 = scatter_all(gr0.reshape(2, 2, 4, 4, 32, PACK), y4, gin4, sums4)
     own_perm = lax.dynamic_index_in_dim(perm, col, 0, keepdims=False).astype(F32)
     vg = lax.dot_general(
         sums4, own_perm, (((1,), (1,)), ((), ())),
         preferred_element_type=F32, precision=lax.Precision.HIGHEST,
     )
-    s0, s1, s2 = (unpacked_block(sums[n]) for n in range(3))
+    s0, s1, s2 = (unpacked_block(part) for part in (late, early[:, :PACK], early[:, PACK:]))
     return (
         layer_output.T,
         gin.T.astype(F32),

time: 369 us -> 357 us (0.967)
  Pallas kernels: 331 us -> 314 us
    pallas_call x1, Pallas kernels: 12.3 us -> 77.5 us  [attend_back_call(): pl.pallas_call(attend_back_kernel, out_shape=(jax.ShapeDtypeStruct((16, 1...]
    pallas_call x1, Pallas kernels: 83.4 us -> 36.2 us  [scatter_all(): pl.pallas_call(scatter_kernel, out_shape=(jax.ShapeDtypeStruct((32, PACK)...]
    pallas_call x4 -> x2, Pallas kernels: 71.7 us -> 37.1 us  [exchange_call(): pl.pallas_call(kernel, out_shape=outs, in_specs=in_specs or [ANY] * len(a...]
where the time goes in v1:
time: 357 us; the launch traced here: 352 us
  Pallas kernels  314 us (88%)
  local copies, waits for them, and re-layouts  23.6 us (7%)
  other arithmetic  11.6 us (3%)
    pallas_call x1, Pallas kernels, attend_back_call(): pl.pallas_call(attend_back_kernel, out_shape=(jax.ShapeDtypeStruct((16, 1...  77.5 us
    pallas_call x1, Pallas kernels, gather_all(): pl.pallas_call(gather_kernel, out_shape=(whole, whole, whole, tokens, tok...  73.9 us
    pallas_call x1, Pallas kernels, middle_call(): pl.pallas_call(middle_kernel, out_shape=(jax.ShapeDtypeStruct((4, 272, QU...  46.4 us
    pallas_call x2, Pallas kernels, exchange_call(): pl.pallas_call(kernel, out_shape=outs, in_specs=in_specs or [ANY] * len(a...  37.1 us
    pallas_call x1, Pallas kernels, scatter_all(): pl.pallas_call(scatter_kernel, out_shape=(jax.ShapeDtypeStruct((32, PACK)...  36.2 us
    pallas_call x1, Pallas kernels, first_call(): pl.pallas_call(first_kernel, out_shape=(jax.ShapeDtypeStruct((4, 272, QUA...  18.6 us
    pallas_call x1, Pallas kernels, qkv_call(): pl.pallas_call(qkv_kernel, out_shape=(row, row, jax.ShapeDtypeStruct((8,...  14.2 us
    pallas_call x1, Pallas kernels, attend_call(): pl.pallas_call(attend_kernel, out_shape=(jax.ShapeDtypeStruct((8, 128, 12...  10.2 us

profile of v1, /device:TPU:1, one launch (start us, length us, event | category | flops | bytes accessed | tf_op | source)
XLA Modules:
  0.0 351.8 jit_solution(5405977086916386860)
XLA Ops:
  4.0 0.8 fusion.23
  4.8 0.7 slice.116
  5.6 0.7 slice.90
  7.0 0.9 fusion.14
  7.9 0.9 slice.115
  9.4 0.9 slice.89
  11.0 2.4 iota_compare_fusion
  13.4 73.9 %gather_weights.1 = (bf16[2,2,4,4,32,1280]{5,4,3,2,1,0:T(8,128)(2,1)}, bf16[2,2,4,4,32,1280]{5,4,3,2,1,0:T(8,128)(2,1)}, bf16[2,2,4,4,32,1280]{5,4,3,2,1,0:T(8,1...) custom-call(bf16[32,1280]{1,0:T(8,128)(2,1)} %get-tuple-element.109.block0, ...), custom_call_target="tpu_custom_call" | custom-call | tf_op jit(solution)/shard_map/gather_weights/pallas_call | solution.py:232
  87.3 14.2 %norm_and_qkv.1 = (bf16[256,1152]{1,0:T(8,128)(2,1)}, bf16[256,1152]{1,0:T(8,128)(2,1)}, f32[8,1152]{1,0:T(8,128)}, bf16[16,192,128]{2,1,0:T(8,128)(2,1)}, bf16[...) custom-call(bf16[4,272,256]{2,1,0:T(8,128)(2,1)} %get-tuple-element.52.x4, f32[4,8,272]{2,1,0:T(8,128)} %get-tuple-element.53.v4, ...), custom_call_target="tpu_custom_call" | custom-call | tf_op jit(solution)/shard_map/norm_and_qkv/pallas_call | solution.py:816
  101.5 21.7 %exchange_qkv.1 = (bf16[16,192,128]{2,1,0:T(8,128)(2,1)}, bf16[16,128,128]{2,1,0:T(8,128)(2,1)}) custom-call(bf16[16,192,128]{2,1,0:T(8,128)(2,1)} %get-tuple-element.57.source, bf16[128,128]{1,0:T(8,128)(2,1)} %get-tuple-element.58.last), custom_call_target="tpu_custom_call" | custom-call | tf_op jit(solution)/shard_map/exchange_qkv/pallas_call | solution.py:323
  123.2 10.2 %attend_forward.1 = (bf16[8,128,128]{2,1,0:T(8,128)(2,1)}, bf16[2048,64]{1,0:T(8,128)(2,1)}, bf16[128,64]{1,0:T(8,128)(2,1)}, f32[1,2048]{1,0:T(1,128)}, f32[1,1...) custom-call(s32[2]{0:T(128)} %pad_add_fusion.info, ...), custom_call_target="tpu_custom_call" | custom-call | tf_op jit(solution)/shard_map/attend_forward/pallas_call | solution.py:1174
  133.3 15.4 %exchange_mixed.1 = (bf16[16,128,128]{2,1,0:T(8,128)(2,1)}, bf16[2,128,64]{2,1,0:T(8,128)(2,1)}) custom-call(bf16[8,128,128]{2,1,0:T(8,128)(2,1)} %get-tuple-element.62.source, bf16[128,64]{1,0:T(8,128)(2,1)} %get-tuple-element.63.last.o16), custom_call_target="tpu_custom_call" | custom-call | tf_op jit(solution)/shard_map/exchange_mixed/pallas_call | solution.py:323
  148.8 1.3 copy.20
  151.2 1.3 pad.47.a0
  152.4 46.4 %feed_forward.1 = (bf16[4,272,128]{2,1,0:T(8,128)(2,1)}, f32[256,1152]{1,0:T(8,128)}, bf16[256,1152]{1,0:T(8,128)(2,1)}, bf16[2,1024,2560]{2,1,0:T(8,128)(2,1)},...) custom-call(bf16[256,1152]{1,0:T(8,128)(2,1)} %get-tuple-element.55.x_ref, ...), custom_call_target="tpu_custom_call" | custom-call | tf_op jit(solution)/shard_map/feed_forward/pallas_call | solution.py:984
  198.8 77.5 %attend_backward.1 = (bf16[16,192,128]{2,1,0:T(8,128)(2,1)}, bf16[8,128,128]{2,1,0:T(8,128)(2,1)}, bf16[128,64]{1,0:T(8,128)(2,1)}, f32[32,2560]{1,0:T(8,128)}) custom-call(bf16[16,64,128]{2,1,0:T(8,128)(2,1)} %get-tuple-element.72.dmsg, bf16[2,2,4,4,32,2560]{5,4,3,2,1,0:T(8,128)(2,1)} %bitcast.55, bf16[2048,64]{1,0:T(8,128)(2,1)} %get-tuple-element.74.query, ...), custom_call_target="tpu_custom_call" | custom-call | tf_op jit(solution)/shard_map/attend_backward/pallas_call | solution.py:1336
  276.4 0.7 fusion.27
  277.1 1.0 fusion.26
  278.1 0.7 pad_maximum_fusion.1
  279.5 1.0 reduce_sum.12
  280.6 3.2 reshape.137
  283.8 1.0 copy.30
  286.6 0.8 copy.25
  288.0 1.1 pad.48.dq_ref
  289.2 18.6 %first_norm_back.1 = (bf16[4,272,128]{2,1,0:T(8,128)(2,1)}, bf16[2,1024,1280]{2,1,0:T(8,128)(2,1)}, f32[8,1152]{1,0:T(8,128)}) custom-call(bf16[256,1152]{1,0:T(8,128)(2,1)} %get-tuple-element.55.x_ref, bf16[256,1152]{1,0:T(8,128)(2,1)} %get-tuple-element.56.n1, bf16[256,1152]{1,0:T(8,128)(2,1)} %get-tuple-element.70.dresb, ...), custom_call_target="tpu_custom_call" | custom-call | tf_op jit(solution)/shard_map/first_norm_back/pallas_call | solution.py:1076
  307.7 36.2 %scatter_gradients.1 = (f32[32,1280]{1,0:T(8,128)}, bf16[272,512]{1,0:T(8,128)(2,1)}, bf16[272,512]{1,0:T(8,128)(2,1)}, f32[8,1152]{1,0:T(8,128)}) custom-call(bf16[2,2,4,4,32,1280]{5,4,3,2,1,0:T(8,128)(2,1)} %bitcast.57, bf16[4,272,128]{2,1,0:T(8,128)(2,1)} %get-tuple-element.86.y_ref, bf16[4,272,128]{2,1,0:T(8,128)(2,1)} %get-tuple-element.87.gin_ref, ...), custom_call_target="tpu_custom_call" | custom-call | tf_op jit(solution)/shard_map/scatter_gradients/pallas_call | solution.py:652
  344.0 1.4 fusion
  346.0 0.7 slice.101
  346.7 0.9 slice.100
  347.7 0.7 fusion.15
  349.1 1.8 convert_bitcast_fusion
  350.9 0.7 copy.33
  (40 shorter events, 10.8 us)
Async XLA Ops:
  148.7 2.0 copy-start.1
  285.1 1.1 copy-start.2
  344.0 6.9 %copy-start = (bf16[272,512]{1,0:T(8,128)(2,1)S(1)}, bf16[272,512]{1,0:T(8,128)(2,1)}, u32[]{:S(2)}) copy-start(bf16[272,512]{1,0:T(8,128)(2,1)} %get-tuple-element.89) | copy-start | bytes 835588
